TPU v7x, 32 devices: a whole 2x2x4 slice. The times are simulated.
32 devices in a mesh: inst: 4 (over z), span: 2 (over x), chord: 4 (over y, core).
Axes of the slice: x: 2, y: 2, z: 4, core: 2. Of those that a mesh axis runs over, the one named last changes fastest.
Arguments:
- adj_source: float32 [4, 8, 32, 1920], P('inst', 'span', 'chord'), may hold values from -6 to 6
- adj_start: float32 [4, 8, 32, 1920], P('inst', 'span', 'chord'), may hold values from -4 to 4
- tiles: bfloat16 [4, 8, 32, 4, 6, 1920], P('inst', 'span', 'chord'), may hold values from -1.25 to 1.25
- tile_cols: int32 [8, 32, 4], P('span', 'chord'), may hold values from 0 to 8, as said below
- inverse_diag: bfloat16 [4, 8, 32, 6, 1920], P('inst', 'span', 'chord'), as said below
- face_src: int32 [2, 2048], P(None, ('span', 'chord')), may hold values from 0 to 10239, as said below
- face_dst: int32 [2, 2048], P(None, ('span', 'chord')), may hold values from 0 to 10239, as said below
- lag_coef: bfloat16 [4, 72, 2048], P('inst', None, ('span', 'chord')), may hold values from -2.5 to 2.5
Outputs:
- adjoint: float32 [4, 8, 32, 1920], P('inst', 'span', 'chord')
- residual: float32 [4, 8, 32, 1920], P('inst', 'span', 'chord')
Inputs may be any that keep to these rules, and one draw needn't show every extreme that they name: `tile_cols`: each block row names code 4 (its own block) once and three distinct other codes; code 3 a + b means the block a - 1 spanwise and b - 1 chordwise away. `face_src`: for each side, the 256 entries of one span and chord group are distinct cell numbers of that group. `face_dst`: for each side, the 256 entries of one span and chord group are distinct cell numbers of that group. `inverse_diag`: diagonal entries of each 6 x 6 block lie in 0.4 to 1.6, off-diagonal entries in -0.35 to 0.35.
All inputs are finite; a program needn't handle non-finite values.
Results may differ from a plain program's by a relative error of at most 0.0003.
Values sent between devices are 32-bit elements; how exact they have to be, the bound alone decides.
A program may use at most 64 MiB of HBM per device.

v0:
```python
import math

import jax
import jax.numpy as jnp
from jax import lax
from jax.sharding import PartitionSpec as P

NV = 6
BLK = 320
SB = 4
CB = 8
PF = 256
SWEEPS = 2
BLADES = 4


rotor_rate = 0.25
spectral_viscosity = 0.03
highest = lax.Precision.HIGHEST


def with_halo(block, sides, width, periodic):
    for axis, dim in sides:
        count = lax.axis_size(axis)
        forward = [(i, i + 1) for i in range(count - 1)]
        if periodic:
            forward.append((count - 1, 0))
        backward = [(target, source) for source, target in forward]
        low = lax.ppermute(
            lax.slice_in_dim(block, block.shape[dim] - width, None, axis=dim), axis, forward
        )
        high = lax.ppermute(lax.slice_in_dim(block, 0, width, axis=dim), axis, backward)
        block = jnp.concatenate([low, block, high], axis=dim)
    return block


def from_behind(array, axis, by):
    peers = lax.axis_size(axis)
    return lax.ppermute(array, axis, [(i, (i + by) % peers) for i in range(peers)])


def spectral_row(instance, total):
    others = jnp.arange(total, dtype=jnp.int32)
    offset = jnp.mod(others - instance, total)
    angle = math.pi / total * offset.astype(jnp.float32)
    parity = jnp.where(jnp.mod(offset, 2) == 0, 1.0, -1.0).astype(jnp.float32)
    sine = jnp.where(offset == 0, 1.0, jnp.sin(angle))
    first = jnp.where(offset == 0, 0.0, 0.5 * parity * jnp.cos(angle) / sine)
    second = jnp.where(offset == 0, -(total * total + 2) / 12.0, -0.5 * parity / (sine * sine))
    return rotor_rate * first - spectral_viscosity * second


def tile_product(extended, tiles, tile_cols):
    rows = tile_cols.shape[0]
    cols = tile_cols.shape[1]
    width = extended.shape[-1]
    selected = jnp.zeros((rows, cols, tile_cols.shape[2], width), jnp.float32)
    for code in range(9):
        view = extended[code // 3 : code // 3 + rows, code % 3 : code % 3 + cols]
        selected = selected + jnp.where((tile_cols == code)[..., None], view[:, :, None, :], 0.0)
    cells = width // NV
    coupled = tiles.astype(jnp.float32).reshape(
        rows, cols, tile_cols.shape[2], NV, NV, cells
    ) * selected.reshape(rows, cols, tile_cols.shape[2], 1, NV, cells)
    return jnp.sum(coupled, axis=(2, 4)).reshape(rows, cols, width)


def lag_pack(blocks, faces):
    return blocks[faces // BLK, :, faces % BLK].T


def lag_apply(pack_behind, pack_ahead, coef, dst_behind, dst_ahead):
    coupling = coef.astype(jnp.float32).reshape(2, NV, NV, PF)
    term = jnp.zeros((SB * CB, NV, BLK), jnp.float32)
    for direction, packed, target in ((0, pack_behind, dst_behind), (1, pack_ahead, dst_ahead)):
        contrib = jnp.sum(coupling[direction] * packed[None, :, :], axis=1)
        term = term.at[target // BLK, :, target % BLK].add(contrib.T)
    return term


def precondition(inverse, residual):
    lead = residual.shape[:-1]
    product = inverse.astype(jnp.float32).reshape(lead + (NV, NV, BLK)) * residual.reshape(
        lead + (1, NV, BLK)
    )
    return jnp.sum(product, axis=-2).reshape(lead + (NV * BLK,))


def per_device(adj_source, adj_start, tiles, tile_cols, inverse_diag, face_src, face_dst, lag_coef):
    instance = lax.axis_index("inst")
    total = lax.axis_size("inst")
    lag = total // BLADES
    source = adj_source[0]
    state = adj_start[0]
    rows, cols, width = state.shape
    own_tiles = tiles[0]
    own_inverse = inverse_diag[0]
    own_coef = lag_coef[0]
    weights = spectral_row(instance, total)
    residual = source
    for sweep_index in range(SWEEPS):
        chord_wide = with_halo(state, (("chord", 1),), 1, True)
        extended = with_halo(chord_wide, (("span", 0),), 1, False)
        blocks = state.reshape(rows * cols, NV, BLK)
        pack_behind = lag_pack(blocks, face_src[0])
        pack_ahead = lag_pack(blocks, face_src[1])
        recv_behind = from_behind(pack_behind, "inst", lag)
        recv_ahead = from_behind(pack_ahead, "inst", -lag)
        spectral_term = jnp.einsum(
            "s,spqf->pqf",
            weights,
            lax.all_gather(state[None], "inst", axis=0, tiled=True),
            precision=highest,
        )
        tile_term = tile_product(extended, own_tiles, tile_cols)
        lag_term = lag_apply(recv_behind, recv_ahead, own_coef, face_dst[0], face_dst[1]).reshape(
            rows, cols, width
        )
        residual = source - (tile_term + spectral_term + lag_term)
        state = state + precondition(own_inverse, residual)
    return (state[None], residual[None])


def solution(mesh):
    return jax.shard_map(
        per_device,
        mesh=mesh,
        in_specs=(
            P("inst", "span", "chord", None),
            P("inst", "span", "chord", None),
            P("inst", "span", "chord", None, None, None),
            P("span", "chord", None),
            P("inst", "span", "chord", None, None),
            P(None, ("span", "chord")),
            P(None, ("span", "chord")),
            P("inst", None, ("span", "chord")),
        ),
        out_specs=(P("inst", "span", "chord", None), P("inst", "span", "chord", None)),
        check_vma=False,
    )
```

profile of v0, /device:TPU:0, one launch (start us, length us, event | category | flops | bytes accessed | tf_op | source)
XLA Modules:
  0.0 273.0 jit_solution(2606638660210209450)
XLA Ops:
  0.7 1.8 fusion.63
  2.9 2.0 collective-permute-start.1
  4.9 1.1 reshape_squeeze.3
  6.0 3.1 %copy.55 = f32[32,6,320]{1,2,0:T(8,128)} copy(f32[32,6,320]{2,1,0:T(8,128)S(1)} %reshape_squeeze.3) | data formatting | bytes 491520 | tf_op jit(solution)/shard_map/reshape;squeeze | solution.py:104
  9.2 3.0 %gather_fusion = f32[256,6]{1,0:T(8,128)} fusion(f32[32,6,320]{1,2,0:T(8,128)} %copy.55, s32[256]{0:T(256)S(1)} %bitcast.105), kind=kCustom, calls=%fused_computation | custom fusion | bytes 14336 | tf_op jit(solution)/shard_map/gather | solution.py:69
  12.1 2.4 collective-permute-start.4
  14.5 3.0 %gather_fusion.1 = f32[256,6]{1,0:T(8,128)} fusion(f32[32,6,320]{1,2,0:T(8,128)} %copy.55, s32[256]{0:T(256)S(1)} %bitcast.103), kind=kCustom, calls=%fused_computation.1 | custom fusion | bytes 14336 | tf_op jit(solution)/shard_map/gather | solution.py:69
  17.4 2.0 collective-permute-start.5
  19.5 20.7 %all_gather.6 = f32[4,4,8,1920]{3,2,1,0:T(8,128)S(1)} all-gather(f32[1,4,8,1920]{3,2,1,0:T(8,128)S(1)} %copy-done), channel_id=1, replica_groups=mesh['inst'=4,'span'=2,'chord'=4] {'inst'}, dimensions={0}, use_global_device_ids=true | all-gather | bytes 1228800 | tf_op jit(solution)/shard_map/all_gather | solution.py:112
  40.2 3.0 %fusion.4 = f32[1,4,8,1920]{3,0,2,1:T(1,128)} fusion(f32[4,4,8,1920]{3,2,1,0:T(8,128)S(1)} %all_gather.6, s32[]{:T(128)S(6)} %axis_index.15), kind=kOutput, calls=%fused_computation.17 | convolution fusion | flops 2949280 | bytes 1228804 | tf_op jit(solution)/shard_map/s,spqf->pqf/dot_general | solution.py:109
  45.8 1.0 copy.56
  46.8 1.0 copy.59
  48.1 3.0 %broadcast.699.clone = f32[32,6,320]{1,2,0:T(8,128)} broadcast(f32[]{:T(128)} %constant.103.clone.1), dimensions={} | broadcast | bytes 245764 | tf_op jit(solution)/shard_map/broadcast.23
  51.1 25.8 %scatter_fusion = f32[32,6,320]{1,2,0:T(8,128)} fusion(f32[32,6,320]{1,2,0:T(8,128)} %broadcast.699.clone, s32[256]{0:T(256)S(1)} %bitcast.109, f32[256,6]{1,0:T(8,128)S(1)} %copy.57), kind=kCustom, calls=%fused_computation.4 | custom fusion | flops 1536 | bytes 20480 | tf_op jit(solution)/shard_map/scatter-add | solution.py:77
  76.9 25.9 %scatter_fusion.1 = f32[32,6,320]{1,2,0:T(8,128)} fusion(f32[32,6,320]{1,2,0:T(8,128)} %scatter_fusion, s32[256]{0:T(256)S(1)} %bitcast.107, f32[256,6]{1,0:T(8,128)S(1)} %copy.60), kind=kCustom, calls=%fused_computation.5 | custom fusion | flops 1536 | bytes 20480 | tf_op jit(solution)/shard_map/scatter-add | solution.py:77
  102.8 3.6 %copy.61 = f32[32,6,320]{2,1,0:T(8,128)S(1)} copy(f32[32,6,320]{1,2,0:T(8,128)} %scatter_fusion.1) | data formatting | bytes 491520 | tf_op jit(solution)/shard_map/scatter-add | solution.py:77
  107.3 3.5 %collective-permute-start.2 = (f32[1,10,1920]{2,1,0:T(8,128)S(1)}, f32[1,10,1920]{2,1,0:T(8,128)S(1)}, u32[]{:S(2)}, u32[]{:S(2)}) collective-permute-start(f32[1,10,1920]{2,1,0:T(8,128)S(1)} %get-tuple-element.20), channel_id=1, source_target_pairs={{0,4},{1,5},{2,6},{3,7},{8,12},{9,13},{10,14},{11,15},{16,20},{17,... | collective-permute-start | bytes 230408 | tf_op jit(solution)/shard_map/ppermute | solution.py:29
  110.8 1.5 collective-permute-start.3
  113.2 4.4 %collective-permute-done.3 = f32[1,10,1920]{2,1,0:T(8,128)S(1)} collective-permute-done((f32[1,10,1920]{2,1,0:T(8,128)S(1)}, f32[1,10,1920]{2,1,0:T(8,128)S(1)}, u32[]{:S(2)}, u32[]{:S(2)}) %collective-permute-start.3) | collective-permute-done | bytes 76832 | tf_op jit(solution)/shard_map/ppermute | solution.py:32
  117.9 1.8 select_add_fusion.1
  119.8 4.2 %fusion = f32[4,8,6,1920]{3,2,1,0:T(8,128)S(1)} fusion(bf16[1,4,8,4,6,1920]{5,3,4,2,1,0:T(4,128)(2,1)S(1)} %copy-done.1, f32[4,8,4,1920]{3,2,1,0:T(4,128)S(1)} %select_add_fusion.1), kind=kLoop, calls=%fused_computation.10 | loop fusion | flops 4055040 | bytes 5406720 | tf_op jit(solution)/shard_map/reduce_sum | solution.py:65
  123.9 1.4 copy.53
  125.4 3.0 %reduce_sum.87 = f32[4,8,6,6,320]{4,3,1,2,0:T(8,128)} reshape(f32[4,8,6,1920]{3,1,2,0:T(8,128)} %copy.53) | data formatting | bytes 2949120 | tf_op jit(solution)/shard_map/reduce_sum | solution.py:65
  128.4 2.4 reduce_sum.88
  131.0 1.8 fusion.9
  132.8 1.1 mul.112
  134.8 3.2 %copy.66 = f32[4,8,6,320]{2,3,1,0:T(8,128)} copy(f32[4,8,6,320]{3,1,2,0:T(8,128)S(1)} %multiply_reduce_fusion.1) | data formatting | bytes 491520 | tf_op jit(solution)/shard_map/reduce_sum | solution.py:86
  138.0 7.2 %bitcast_add_fusion = f32[32,6,320]{1,2,0:T(8,128)} fusion(f32[32,6,320]{1,2,0:T(8,128)} %copy.55, f32[4,8,6,320]{2,3,1,0:T(8,128)} %copy.66), kind=kLoop, calls=%fused_computation.12 | loop fusion | flops 61440 | bytes 737280 | tf_op jit(solution)/shard_map/add | solution.py:120
  145.2 3.0 %gather_fusion.2 = f32[256,6]{1,0:T(8,128)} fusion(f32[32,6,320]{1,2,0:T(8,128)} %bitcast_add_fusion, s32[256]{0:T(256)S(1)} %bitcast.106), kind=kCustom, calls=%fused_computation.2 | custom fusion | bytes 14336 | tf_op jit(solution)/shard_map/gather | solution.py:69
  148.2 3.0 %gather_fusion.3 = f32[256,6]{1,0:T(8,128)} fusion(f32[32,6,320]{1,2,0:T(8,128)} %bitcast_add_fusion, s32[256]{0:T(256)S(1)} %bitcast.104), kind=kCustom, calls=%fused_computation.3 | custom fusion | bytes 14336 | tf_op jit(solution)/shard_map/gather | solution.py:69
  153.7 1.7 collective-permute-start.7
  155.7 3.5 %collective-permute-start.11 = (f32[6,256]{0,1:T(8,128)}, f32[6,256]{0,1:T(8,128)}, u32[]{:S(2)}, u32[]{:S(2)}) collective-permute-start(f32[6,256]{0,1:T(8,128)} %bitcast.117), channel_id=1, source_target_pairs={{0,24},{8,0},{16,8},{24,16},{1,25},{9,1},{17,9},{25,17},{2,26},{10... | collective-permute-start | bytes 18440 | tf_op jit(solution)/shard_map/ppermute | solution.py:39
  159.3 22.1 %all_gather.7 = f32[4,4,8,1920]{3,2,1,0:T(8,128)S(1)} all-gather(f32[1,4,8,1920]{3,2,1,0:T(8,128)S(1)} %add.359), channel_id=1, replica_groups=mesh['inst'=4,'span'=2,'chord'=4] {'inst'}, dimensions={0}, use_global_device_ids=true | all-gather | bytes 1228800 | tf_op jit(solution)/shard_map/all_gather | solution.py:112
  181.3 3.0 %fusion.2 = f32[1,4,8,1920]{3,0,2,1:T(1,128)} fusion(f32[4,4,8,1920]{3,2,1,0:T(8,128)S(1)} %all_gather.7, s32[]{:T(128)S(6)} %axis_index.15), kind=kOutput, calls=%fused_computation.15 | convolution fusion | flops 2949280 | bytes 1228804 | tf_op jit(solution)/shard_map/s,spqf->pqf/dot_general | solution.py:109
  185.3 1.0 copy.70
  186.7 2.9 %broadcast.699 = f32[32,6,320]{1,2,0:T(8,128)} broadcast(f32[]{:T(128)} %constant.103.clone.1), dimensions={} | broadcast | bytes 245764 | tf_op jit(solution)/shard_map/broadcast.23
  189.6 25.8 %scatter_fusion.2 = f32[32,6,320]{1,2,0:T(8,128)} fusion(f32[32,6,320]{1,2,0:T(8,128)} %broadcast.699, s32[256]{0:T(256)S(1)} %bitcast.110, f32[256,6]{1,0:T(8,128)S(1)} %copy.69), kind=kCustom, calls=%fused_computation.6 | custom fusion | flops 1536 | bytes 20480 | tf_op jit(solution)/shard_map/scatter-add | solution.py:77
  215.4 25.8 %scatter_fusion.3 = f32[32,6,320]{1,2,0:T(8,128)} fusion(f32[32,6,320]{1,2,0:T(8,128)} %scatter_fusion.2, s32[256]{0:T(256)S(1)} %bitcast.108, f32[256,6]{1,0:T(8,128)S(1)} %copy.71), kind=kCustom, calls=%fused_computation.7 | custom fusion | flops 1536 | bytes 20480 | tf_op jit(solution)/shard_map/scatter-add | solution.py:77
  241.3 3.6 %copy.72 = f32[32,6,320]{2,1,0:T(8,128)S(1)} copy(f32[32,6,320]{1,2,0:T(8,128)} %scatter_fusion.3) | data formatting | bytes 491520 | tf_op jit(solution)/shard_map/scatter-add | solution.py:77
  246.6 1.4 collective-permute-start.8
  248.0 1.3 collective-permute-start.9
  250.5 4.4 %collective-permute-done.9 = f32[1,10,1920]{2,1,0:T(8,128)S(1)} collective-permute-done((f32[1,10,1920]{2,1,0:T(8,128)S(1)}, f32[1,10,1920]{2,1,0:T(8,128)S(1)}, u32[]{:S(2)}, u32[]{:S(2)}) %collective-permute-start.9) | collective-permute-done | bytes 76832 | tf_op jit(solution)/shard_map/ppermute | solution.py:32
  256.0 1.9 select_add_fusion
  257.9 4.2 %fusion.1 = f32[4,8,6,1920]{3,2,1,0:T(8,128)S(1)} fusion(bf16[1,4,8,4,6,1920]{5,3,4,2,1,0:T(4,128)(2,1)S(1)} %copy-done.2, f32[4,8,4,1920]{3,2,1,0:T(4,128)S(1)} %select_add_fusion), kind=kLoop, calls=%fused_computation.11 | loop fusion | flops 4055040 | bytes 5406720 | tf_op jit(solution)/shard_map/reduce_sum | solution.py:65
  262.0 1.4 copy.64
  263.4 3.0 %reduce_sum.93 = f32[4,8,6,6,320]{4,3,1,2,0:T(8,128)} reshape(f32[4,8,6,1920]{3,1,2,0:T(8,128)} %copy.64) | data formatting | bytes 2949120 | tf_op jit(solution)/shard_map/reduce_sum | solution.py:65
  266.4 2.4 reduce_sum.94
  269.7 1.4 fusion.7
  (129 shorter events, 17.4 us)
Async XLA Ops:
  0.6 18.8 %copy-start = (f32[1,4,8,1920]{3,2,1,0:T(8,128)S(1)}, f32[1,4,8,1920]{3,2,1,0:T(8,128)}, u32[]{:S(2)}) copy-start(f32[1,4,8,1920]{3,2,1,0:T(8,128)} %param.9) | copy-start | bytes 737284
  0.6 8.5 %copy-start.30 = (s32[2,256]{1,0:T(2,128)S(1)}, s32[2,256]{1,0:T(2,128)}, u32[]{:S(2)}) copy-start(s32[2,256]{1,0:T(2,128)} %param.13) | copy-start | bytes 6148
  0.7 39.5 %copy-start.29 = (s32[4,8,4]{1,2,0:T(4,128)S(1)}, s32[4,8,4]{1,2,0:T(4,128)}, u32[]{:S(2)}) copy-start(s32[4,8,4]{1,2,0:T(4,128)} %param.11) | copy-start | bytes 1540
  0.7 39.6 %copy-start.10 = (bf16[1,72,256]{2,1,0:T(8,128)(2,1)S(1)}, bf16[1,72,256]{2,1,0:T(8,128)(2,1)}, u32[]{:S(2)}) copy-start(bf16[1,72,256]{2,1,0:T(8,128)(2,1)} %param.15) | copy-start | bytes 110596
  2.5 104.7 %collective-permute-start = (f32[4,1,1920]{2,1,0:T(1,128)}, f32[4,1,1920]{2,1,0:T(1,128)S(1)}, u32[]{:S(2)}, u32[]{:S(2)}) collective-permute-start(f32[4,1,1920]{2,1,0:T(1,128)} %get-tuple-element.28), channel_id=1, source_target_pairs={{0,1},{1,2},{2,3},{3,0},{4,5},{5,6},{6,7},{7,4},{8,9},{9,10},{10,1... | collective-permute-start | bytes 92168 | tf_op jit(solution)/shard_map/ppermute | solution.py:29
  2.9 104.3 %collective-permute-start.1 = (f32[4,1,1920]{2,1,0:T(1,128)}, f32[4,1,1920]{2,1,0:T(1,128)S(1)}, u32[]{:S(2)}, u32[]{:S(2)}) collective-permute-start(f32[4,1,1920]{2,1,0:T(1,128)} %get-tuple-element.29), channel_id=1, source_target_pairs={{1,0},{2,1},{3,2},{0,3},{5,4},{6,5},{7,6},{4,7},{9,8},{10,9},{11,1... | collective-permute-start | bytes 92168 | tf_op jit(solution)/shard_map/ppermute | solution.py:32
  6.0 37.2 %copy-start.31 = (s32[2,256]{1,0:T(2,128)S(1)}, s32[2,256]{1,0:T(2,128)}, u32[]{:S(2)}) copy-start(s32[2,256]{1,0:T(2,128)} %param.14) | copy-start | bytes 6148
  6.0 38.9 %copy-start.5 = (bf16[1,4,8,6,1920]{4,2,3,1,0:T(8,128)(2,1)S(1)}, bf16[1,4,8,6,1920]{4,2,3,1,0:T(8,128)(2,1)}, u32[]{:S(2)}) copy-start(bf16[1,4,8,6,1920]{4,2,3,1,0:T(8,128)(2,1)} %param.12) | copy-start | bytes 2211844
  12.1 33.6 %collective-permute-start.4 = (f32[6,256]{0,1:T(8,128)}, f32[6,256]{0,1:T(8,128)}, u32[]{:S(2)}, u32[]{:S(2)}) collective-permute-start(f32[6,256]{0,1:T(8,128)} %bitcast.13), channel_id=1, source_target_pairs={{0,8},{8,16},{16,24},{24,0},{1,9},{9,17},{17,25},{25,1},{2,10},{10... | collective-permute-start | bytes 18440 | tf_op jit(solution)/shard_map/ppermute | solution.py:39
  17.4 29.3 %collective-permute-start.5 = (f32[6,256]{0,1:T(8,128)}, f32[6,256]{0,1:T(8,128)}, u32[]{:S(2)}, u32[]{:S(2)}) collective-permute-start(f32[6,256]{0,1:T(8,128)} %bitcast.23), channel_id=1, source_target_pairs={{0,24},{8,0},{16,8},{24,16},{1,25},{9,1},{17,9},{25,17},{2,26},{10... | collective-permute-start | bytes 18440 | tf_op jit(solution)/shard_map/ppermute | solution.py:39
  43.4 74.5 %copy-start.11 = (pred[4,8,4]{2,1,0:T(8,128)(4,1)}, pred[4,8,4]{2,1,0:T(8,128)(4,1)S(1)}, u32[]{:S(2)}) copy-start(pred[4,8,4]{2,1,0:T(8,128)(4,1)S(1)} %copy.44) | copy-start | bytes 388
  43.5 74.4 %copy-start.13 = (pred[4,8,4]{2,1,0:T(8,128)(4,1)}, pred[4,8,4]{2,1,0:T(8,128)(4,1)S(1)}, u32[]{:S(2)}) copy-start(pred[4,8,4]{2,1,0:T(8,128)(4,1)S(1)} %copy.45) | copy-start | bytes 388
  43.6 74.3 %copy-start.15 = (pred[4,8,4]{2,1,0:T(8,128)(4,1)}, pred[4,8,4]{2,1,0:T(8,128)(4,1)S(1)}, u32[]{:S(2)}) copy-start(pred[4,8,4]{2,1,0:T(8,128)(4,1)S(1)} %copy.46) | copy-start | bytes 388
  43.7 74.2 %copy-start.17 = (pred[4,8,4]{2,1,0:T(8,128)(4,1)}, pred[4,8,4]{2,1,0:T(8,128)(4,1)S(1)}, u32[]{:S(2)}) copy-start(pred[4,8,4]{2,1,0:T(8,128)(4,1)S(1)} %copy.47) | copy-start | bytes 388
  43.8 74.0 %copy-start.19 = (pred[4,8,4]{2,1,0:T(8,128)(4,1)}, pred[4,8,4]{2,1,0:T(8,128)(4,1)S(1)}, u32[]{:S(2)}) copy-start(pred[4,8,4]{2,1,0:T(8,128)(4,1)S(1)} %copy.48) | copy-start | bytes 388
  43.9 73.9 %copy-start.21 = (pred[4,8,4]{2,1,0:T(8,128)(4,1)}, pred[4,8,4]{2,1,0:T(8,128)(4,1)S(1)}, u32[]{:S(2)}) copy-start(pred[4,8,4]{2,1,0:T(8,128)(4,1)S(1)} %copy.49) | copy-start | bytes 388
  44.0 73.8 %copy-start.23 = (pred[4,8,4]{2,1,0:T(8,128)(4,1)}, pred[4,8,4]{2,1,0:T(8,128)(4,1)S(1)}, u32[]{:S(2)}) copy-start(pred[4,8,4]{2,1,0:T(8,128)(4,1)S(1)} %copy.50) | copy-start | bytes 388
  44.2 73.7 %copy-start.25 = (pred[4,8,4]{2,1,0:T(8,128)(4,1)}, pred[4,8,4]{2,1,0:T(8,128)(4,1)S(1)}, u32[]{:S(2)}) copy-start(pred[4,8,4]{2,1,0:T(8,128)(4,1)S(1)} %copy.51) | copy-start | bytes 388
  44.9 61.5 %copy-start.8 = (f32[6,6,256]{2,1,0:T(8,128)}, f32[6,6,256]{2,1,0:T(8,128)S(1)}, u32[]{:S(2)}) copy-start(f32[6,6,256]{2,1,0:T(8,128)S(1)} %squeeze.10) | copy-start | bytes 110596
  44.9 61.5 %copy-start.6 = (f32[6,6,256]{2,1,0:T(8,128)}, f32[6,6,256]{2,1,0:T(8,128)S(1)}, u32[]{:S(2)}) copy-start(f32[6,6,256]{2,1,0:T(8,128)S(1)} %squeeze.11) | copy-start | bytes 110596
  102.8 15.1 %copy-start.27 = (pred[4,8,4]{2,1,0:T(8,128)(4,1)S(1)}, pred[4,8,4]{2,1,0:T(8,128)(4,1)}, u32[]{:S(2)}) copy-start(pred[4,8,4]{2,1,0:T(8,128)(4,1)} %copy.52) | copy-start | bytes 388
  107.2 12.6 %copy-start.1 = (bf16[1,4,8,4,6,1920]{5,3,4,2,1,0:T(4,128)(2,1)S(1)}, bf16[1,4,8,4,6,1920]{5,3,4,2,1,0:T(4,128)(2,1)}, u32[]{:S(2)}) copy-start(bf16[1,4,8,4,6,1920]{5,3,4,2,1,0:T(4,128)(2,1)} %param.10) | copy-start | bytes 8847364
  107.3 6.0 %collective-permute-start.2 = (f32[1,10,1920]{2,1,0:T(8,128)S(1)}, f32[1,10,1920]{2,1,0:T(8,128)S(1)}, u32[]{:S(2)}, u32[]{:S(2)}) collective-permute-start(f32[1,10,1920]{2,1,0:T(8,128)S(1)} %get-tuple-element.20), channel_id=1, source_target_pairs={{0,4},{1,5},{2,6},{3,7},{8,12},{9,13},{10,14},{11,15},{16,20},{17,... | collective-permute-start | bytes 230408 | tf_op jit(solution)/shard_map/ppermute | solution.py:29
  110.8 6.8 %collective-permute-start.3 = (f32[1,10,1920]{2,1,0:T(8,128)S(1)}, f32[1,10,1920]{2,1,0:T(8,128)S(1)}, u32[]{:S(2)}, u32[]{:S(2)}) collective-permute-start(f32[1,10,1920]{2,1,0:T(8,128)S(1)} %get-tuple-element.21), channel_id=1, source_target_pairs={{4,0},{5,1},{6,2},{7,3},{12,8},{13,9},{14,10},{15,11},{20,16},{21,... | collective-permute-start | bytes 230408 | tf_op jit(solution)/shard_map/ppermute | solution.py:32
  123.9 7.1 %copy-start.3 = (f32[1,4,8,1920]{3,2,1,0:T(8,128)S(1)}, f32[1,4,8,1920]{3,2,1,0:T(8,128)}, u32[]{:S(2)}) copy-start(f32[1,4,8,1920]{3,2,1,0:T(8,128)} %param.8) | copy-start | bytes 737284
  145.2 40.1 %copy-start.9 = (f32[6,6,256]{2,1,0:T(8,128)S(1)}, f32[6,6,256]{2,1,0:T(8,128)}, u32[]{:S(2)}) copy-start(f32[6,6,256]{2,1,0:T(8,128)} %copy-done.8) | copy-start | bytes 110596
  145.2 41.1 %copy-start.7 = (f32[6,6,256]{2,1,0:T(8,128)S(1)}, f32[6,6,256]{2,1,0:T(8,128)}, u32[]{:S(2)}) copy-start(f32[6,6,256]{2,1,0:T(8,128)} %copy-done.6) | copy-start | bytes 110596
  153.7 92.0 %collective-permute-start.6 = (f32[4,1,1920]{2,1,0:T(1,128)}, f32[4,1,1920]{2,1,0:T(1,128)S(1)}, u32[]{:S(2)}, u32[]{:S(2)}) collective-permute-start(f32[4,1,1920]{2,1,0:T(1,128)} %get-tuple-element.24), channel_id=1, source_target_pairs={{0,1},{1,2},{2,3},{3,0},{4,5},{5,6},{6,7},{7,4},{8,9},{9,10},{10,1... | collective-permute-start | bytes 92168 | tf_op jit(solution)/shard_map/ppermute | solution.py:29
  153.7 92.0 %collective-permute-start.7 = (f32[4,1,1920]{2,1,0:T(1,128)}, f32[4,1,1920]{2,1,0:T(1,128)}, u32[]{:S(2)}, u32[]{:S(2)}) collective-permute-start(f32[4,1,1920]{2,1,0:T(1,128)} %get-tuple-element.25), channel_id=1, source_target_pairs={{1,0},{2,1},{3,2},{0,3},{5,4},{6,5},{7,6},{4,7},{9,8},{10,9},{11,1... | collective-permute-start | bytes 92168 | tf_op jit(solution)/shard_map/ppermute | solution.py:32
  155.4 28.9 %collective-permute-start.10 = (f32[6,256]{0,1:T(8,128)}, f32[6,256]{0,1:T(8,128)}, u32[]{:S(2)}, u32[]{:S(2)}) collective-permute-start(f32[6,256]{0,1:T(8,128)} %bitcast.118), channel_id=1, source_target_pairs={{0,8},{8,16},{16,24},{24,0},{1,9},{9,17},{17,25},{25,1},{2,10},{10... | collective-permute-start | bytes 18440 | tf_op jit(solution)/shard_map/ppermute | solution.py:39
  155.7 29.6 %collective-permute-start.11 = (f32[6,256]{0,1:T(8,128)}, f32[6,256]{0,1:T(8,128)}, u32[]{:S(2)}, u32[]{:S(2)}) collective-permute-start(f32[6,256]{0,1:T(8,128)} %bitcast.117), channel_id=1, source_target_pairs={{0,24},{8,0},{16,8},{24,16},{1,25},{9,1},{17,9},{25,17},{2,26},{10... | collective-permute-start | bytes 18440 | tf_op jit(solution)/shard_map/ppermute | solution.py:39
  241.2 14.7 %copy-start.12 = (pred[4,8,4]{2,1,0:T(8,128)(4,1)S(1)}, pred[4,8,4]{2,1,0:T(8,128)(4,1)}, u32[]{:S(2)}) copy-start(pred[4,8,4]{2,1,0:T(8,128)(4,1)} %copy-done.11) | copy-start | bytes 388
  241.2 14.7 %copy-start.14 = (pred[4,8,4]{2,1,0:T(8,128)(4,1)S(1)}, pred[4,8,4]{2,1,0:T(8,128)(4,1)}, u32[]{:S(2)}) copy-start(pred[4,8,4]{2,1,0:T(8,128)(4,1)} %copy-done.13) | copy-start | bytes 388
  241.2 14.7 %copy-start.16 = (pred[4,8,4]{2,1,0:T(8,128)(4,1)S(1)}, pred[4,8,4]{2,1,0:T(8,128)(4,1)}, u32[]{:S(2)}) copy-start(pred[4,8,4]{2,1,0:T(8,128)(4,1)} %copy-done.15) | copy-start | bytes 388
  241.2 14.7 %copy-start.18 = (pred[4,8,4]{2,1,0:T(8,128)(4,1)S(1)}, pred[4,8,4]{2,1,0:T(8,128)(4,1)}, u32[]{:S(2)}) copy-start(pred[4,8,4]{2,1,0:T(8,128)(4,1)} %copy-done.17) | copy-start | bytes 388
  241.2 14.7 %copy-start.20 = (pred[4,8,4]{2,1,0:T(8,128)(4,1)S(1)}, pred[4,8,4]{2,1,0:T(8,128)(4,1)}, u32[]{:S(2)}) copy-start(pred[4,8,4]{2,1,0:T(8,128)(4,1)} %copy-done.19) | copy-start | bytes 388
  241.2 14.7 %copy-start.22 = (pred[4,8,4]{2,1,0:T(8,128)(4,1)S(1)}, pred[4,8,4]{2,1,0:T(8,128)(4,1)}, u32[]{:S(2)}) copy-start(pred[4,8,4]{2,1,0:T(8,128)(4,1)} %copy-done.21) | copy-start | bytes 388
  241.2 14.7 %copy-start.24 = (pred[4,8,4]{2,1,0:T(8,128)(4,1)S(1)}, pred[4,8,4]{2,1,0:T(8,128)(4,1)}, u32[]{:S(2)}) copy-start(pred[4,8,4]{2,1,0:T(8,128)(4,1)} %copy-done.23) | copy-start | bytes 388
  241.3 14.7 %copy-start.26 = (pred[4,8,4]{2,1,0:T(8,128)(4,1)S(1)}, pred[4,8,4]{2,1,0:T(8,128)(4,1)}, u32[]{:S(2)}) copy-start(pred[4,8,4]{2,1,0:T(8,128)(4,1)} %copy-done.25) | copy-start | bytes 388
  241.3 14.7 %copy-start.28 = (pred[4,8,4]{2,1,0:T(8,128)(4,1)S(1)}, pred[4,8,4]{2,1,0:T(8,128)(4,1)}, u32[]{:S(2)}) copy-start(pred[4,8,4]{2,1,0:T(8,128)(4,1)} %copy.52) | copy-start | bytes 388
  245.7 12.2 %copy-start.2 = (bf16[1,4,8,4,6,1920]{5,3,4,2,1,0:T(4,128)(2,1)S(1)}, bf16[1,4,8,4,6,1920]{5,3,4,2,1,0:T(4,128)(2,1)}, u32[]{:S(2)}) copy-start(bf16[1,4,8,4,6,1920]{5,3,4,2,1,0:T(4,128)(2,1)} %param.10) | copy-start | bytes 8847364
  246.6 3.9 %collective-permute-start.8 = (f32[1,10,1920]{2,1,0:T(8,128)S(1)}, f32[1,10,1920]{2,1,0:T(8,128)S(1)}, u32[]{:S(2)}, u32[]{:S(2)}) collective-permute-start(f32[1,10,1920]{2,1,0:T(8,128)S(1)} %get-tuple-element.16), channel_id=1, source_target_pairs={{0,4},{1,5},{2,6},{3,7},{8,12},{9,13},{10,14},{11,15},{16,20},{17,... | collective-permute-start | bytes 230408 | tf_op jit(solution)/shard_map/ppermute | solution.py:29
  248.0 6.8 %collective-permute-start.9 = (f32[1,10,1920]{2,1,0:T(8,128)S(1)}, f32[1,10,1920]{2,1,0:T(8,128)S(1)}, u32[]{:S(2)}, u32[]{:S(2)}) collective-permute-start(f32[1,10,1920]{2,1,0:T(8,128)S(1)} %get-tuple-element.17), channel_id=1, source_target_pairs={{4,0},{5,1},{6,2},{7,3},{12,8},{13,9},{14,10},{15,11},{20,16},{21,... | collective-permute-start | bytes 230408 | tf_op jit(solution)/shard_map/ppermute | solution.py:32
  271.1 1.9 copy-start.4
where the time goes:
time: 276 us; the launch traced here: 273 us
  other arithmetic  137 us (50%)
  local copies, waits for them, and re-layouts  56.1 us (20%)
  blocking collectives  42.8 us (16%)
  starting transfers between devices  20.1 us (7%)
  waiting for transfers between devices  9.85 us (4%)
  matrix products  5.92 us (2%)
    scatter-add x4, other arithmetic, lag_apply(): term = term.at[target // BLK, :, target % BLK].add(contrib.T)  103 us
    all_gather x2, blocking collectives, per_device(): lax.all_gather(state[None], 'inst', axis=0, tiled=True)  42.8 us
    reduce_sum x4, other arithmetic, tile_product(): return jnp.sum(coupled, axis=(2, 4)).reshape(rows, cols, width)  13.1 us
    gather x4, local copies, waits for them, and re-layouts, lag_pack(): return blocks[faces // BLK, :, faces % BLK].T  11.9 us
    reduce_sum x6, local copies, waits for them, and re-layouts, tile_product(): return jnp.sum(coupled, axis=(2, 4)).reshape(rows, cols, width)  9.05 us
    add x4, other arithmetic, per_device(): state = state + precondition(own_inverse, residual)  8.88 us
    ppermute x4, waiting for transfers between devices, with_halo(): lax.ppermute(lax.slice_in_dim(block, 0, width, axis=dim), axis, backward)  8.71 us
    ppermute x4, starting transfers between devices, from_behind(): lax.ppermute(array, axis, [(i, (i + by) % peers) for i in range(peers)])  8.21 us
  transfers between devices with their start and end apart: 12, of which 4 were waited for; matrix products, arithmetic and copies ran while one was open for 52% of the time, Pallas kernels for 0%

commit v1 on v0

v1 whole, which is shorter than its diff:
```python
import math

import jax
import jax.numpy as jnp
from jax import lax
from jax.experimental import pallas as pl
from jax.experimental.pallas import tpu as pltpu
from jax.sharding import PartitionSpec as P

NV = 6
SWEEPS = 2
BLADES = 4
RIGHT, LEFT = 0, 1

rotor_rate = 0.25
spectral_viscosity = 0.03
MESH = pl.DeviceIdType.MESH


def spectral_weight(offset, total):
    m = offset % total
    if m == 0:
        return spectral_viscosity * (total * total + 2) / 12.0
    parity = -1.0 if m % 2 else 1.0
    angle = math.pi * m / total
    first = 0.5 * parity * math.cos(angle) / math.sin(angle)
    second = -0.5 * parity / math.sin(angle) ** 2
    return rotor_rate * first - spectral_viscosity * second


def split3(x):
    high = x.astype(jnp.bfloat16)
    rest = x - high.astype(jnp.float32)
    middle = rest.astype(jnp.bfloat16)
    low = (rest - middle.astype(jnp.float32)).astype(jnp.bfloat16)
    return jnp.concatenate([high, middle, low], axis=0)


def sum3(y):
    n = y.shape[0] // 3
    return (y[2 * n :] + y[n : 2 * n]) + y[:n]


def make_kernel(sizes, n_inst, n_span, n_chord):
    SB, CB, W, K, PF = sizes
    BLK = W // NV
    PAIR = 2 * BLK
    NP = NV // 2
    BLKS = SB * CB
    EXT = CB + 2
    half = n_inst // 2
    lag = n_inst // BLADES

    def kernel(
        x0_ref, source_ref, cols_ref, fsrc_ref, fdst_ref, coef_ref, tiles_hbm, inv_hbm,
        adj_ref, res_ref,
        tiles_ref, inv_ref, x1_ref, xb_ref, base_ref, g_ref, coef32_ref, oh_src, oh_dst, mask_src, mask_dst,
        gat_ref, sum_ref, col_send, corn_send, col_recv, row_recv, corn_recv, pack_send, pack_recv,
        load_sem, gs_sem, gr_sem, hs_sem, hr_sem, ps_sem, pr_sem,
    ):
        t = lax.axis_index("inst")
        sp = lax.axis_index("span")
        ch = lax.axis_index("chord")
        ch_up = lax.rem(ch + 1, n_chord)
        ch_dn = lax.rem(ch + n_chord - 1, n_chord)
        t_up = lax.rem(t + lag, n_inst)
        t_dn = lax.rem(t + n_inst - lag, n_inst)
        has_lo = sp > 0
        has_hi = sp < n_span - 1

        loads = []
        for p in range(SB):
            loads.append(
                pltpu.make_async_copy(
                    tiles_hbm.at[pl.ds(p * CB, CB)], tiles_ref.at[pl.ds(p * CB, CB)], load_sem.at[p]
                )
            )
        inv_load = pltpu.make_async_copy(inv_hbm, inv_ref, load_sem.at[SB])
        for load in loads:
            load.start()
        inv_load.start()

        barrier = pltpu.get_barrier_semaphore()

        def greet(i, s, c):
            pl.semaphore_signal(barrier, inc=1, device_id=(i, s, c), device_id_type=MESH)

        count = 4 + 3 * jnp.where(has_lo, 1, 0) + 3 * jnp.where(has_hi, 1, 0)
        greet(t_up, sp, ch)
        greet(t_dn, sp, ch)
        greet(t, sp, ch_up)
        greet(t, sp, ch_dn)
        if lag != 1:
            count = count + jnp.where(t > 0, 1, 0) + jnp.where(t < n_inst - 1, 1, 0)

            @pl.when(t > 0)
            def _():
                greet(t - 1, sp, ch)

            @pl.when(t < n_inst - 1)
            def _():
                greet(t + 1, sp, ch)

        @pl.when(has_lo)
        def _():
            for c in (ch, ch_up, ch_dn):
                greet(t, sp - 1, c)

        @pl.when(has_hi)
        def _():
            for c in (ch, ch_up, ch_dn):
                greet(t, sp + 1, c)

        pl.semaphore_wait(barrier, count)

        def at(direction):
            return t if direction == RIGHT else n_inst - 1 - t

        def stream(sweep, direction, j, p, src):
            target = t + 1 if direction == RIGHT else t - 1
            return pltpu.make_async_remote_copy(
                src_ref=src,
                dst_ref=gat_ref.at[sweep, direction, j, p],
                send_sem=gs_sem.at[sweep, direction, j, p],
                recv_sem=gr_sem.at[sweep, direction, j, p],
                device_id=(target, sp, ch),
                device_id_type=MESH,
            )

        def weight(direction, hops):
            return spectral_weight(-hops if direction == RIGHT else hops, n_inst)

        def send_own(sweep, p, x_ref):
            for d in (RIGHT, LEFT):

                @pl.when(at(d) < half)
                def _():
                    stream(sweep, d, 0, p, x_ref.at[p]).start()

        def forward(sweep, p):
            for d in (RIGHT, LEFT):
                for j in range(1, half):

                    @pl.when(jnp.logical_and(at(d) >= j, at(d) < half))
                    def _():
                        got = gat_ref.at[sweep, d, j - 1, p]
                        stream(sweep, d, j - 1, p, got).wait_recv()
                        stream(sweep, d, j, p, got).start()

        def collect(sweep, p, x_ref):
            for d in (RIGHT, LEFT):

                @pl.when(at(d) == half)
                def _():
                    for j in range(half):
                        stream(sweep, d, j, p, gat_ref.at[sweep, d, j, p]).wait_recv()
                    for j in range(n_inst - 1 - half):
                        total = weight(d, 1 + j) * x_ref[p]
                        for i in range(half):
                            total = total + weight(d, 2 + j + i) * gat_ref[sweep, d, i, p]
                        sum_ref[sweep, d, j, p] = total
                        stream(sweep, d, j, p, sum_ref.at[sweep, d, j, p]).start()

                for place in range(half + 1, n_inst):

                    @pl.when(at(d) == place)
                    def _():
                        for j in range(n_inst - place):
                            stream(sweep, d, j, p, gat_ref.at[sweep, d, j, p]).wait_recv()
                        for j in range(n_inst - 1 - place):
                            sum_ref[sweep, d, j, p] = gat_ref[sweep, d, j + 1, p] + weight(d, 1 + j) * x_ref[p]
                            stream(sweep, d, j, p, sum_ref.at[sweep, d, j, p]).start()

        def spectral(sweep, p, x_ref):
            res_ref[p] = base_ref[p] - spectral_weight(0, n_inst) * x_ref[p]
            for d in (RIGHT, LEFT):
                for i in range(half):

                    @pl.when(jnp.logical_and(at(d) > i, at(d) <= half))
                    def _():
                        res_ref[p] = res_ref[p] - weight(d, 1 + i) * gat_ref[sweep, d, i, p]

                @pl.when(at(d) > half)
                def _():
                    res_ref[p] = res_ref[p] - gat_ref[sweep, d, 0, p]

        def drain(sweep, p):
            for d in (RIGHT, LEFT):
                for j in range(half):
                    raw = jnp.logical_and(at(d) < half, at(d) >= j)
                    summed = jnp.logical_and(at(d) >= half, at(d) < n_inst - 1 - j)

                    @pl.when(jnp.logical_or(raw, summed))
                    def _():
                        stream(sweep, d, j, p, gat_ref.at[sweep, d, j, p]).wait_send()

        def halo(sweep, place, src, dst, device):
            return pltpu.make_async_remote_copy(
                src_ref=src,
                dst_ref=dst,
                send_sem=hs_sem.at[sweep, place],
                recv_sem=hr_sem.at[sweep, place],
                device_id=device,
                device_id_type=MESH,
            )

        def columns(sweep):
            return [
                halo(sweep, 0, col_send.at[sweep, 0], col_recv.at[sweep, 0], (t, sp, ch_up)),
                halo(sweep, 1, col_send.at[sweep, 1], col_recv.at[sweep, 1], (t, sp, ch_dn)),
            ]

        def upward(sweep, x_ref):
            return [
                halo(sweep, 2, x_ref.at[SB - 1], row_recv.at[sweep, 0], (t, sp + 1, ch)),
                halo(sweep, 4, corn_send.at[sweep, 0], corn_recv.at[sweep, 0], (t, sp + 1, ch_up)),
                halo(sweep, 5, corn_send.at[sweep, 1], corn_recv.at[sweep, 1], (t, sp + 1, ch_dn)),
            ]

        def downward(sweep, x_ref):
            return [
                halo(sweep, 3, x_ref.at[0], row_recv.at[sweep, 1], (t, sp - 1, ch)),
                halo(sweep, 6, corn_send.at[sweep, 2], corn_recv.at[sweep, 2], (t, sp - 1, ch_up)),
                halo(sweep, 7, corn_send.at[sweep, 3], corn_recv.at[sweep, 3], (t, sp - 1, ch_dn)),
            ]

        def send_halos(sweep, x_ref):
            for p in range(SB):
                col_send[sweep, 0, p : p + 1, :] = x_ref[p, CB - 1 : CB, :]
                col_send[sweep, 1, p : p + 1, :] = x_ref[p, 0:1, :]
            corn_send[sweep, 0] = x_ref[SB - 1, CB - 1 : CB, :]
            corn_send[sweep, 1] = x_ref[SB - 1, 0:1, :]
            corn_send[sweep, 2] = x_ref[0, CB - 1 : CB, :]
            corn_send[sweep, 3] = x_ref[0, 0:1, :]
            for copy in columns(sweep):
                copy.start()

            @pl.when(has_hi)
            def _():
                for copy in upward(sweep, x_ref):
                    copy.start()

            @pl.when(has_lo)
            def _():
                for copy in downward(sweep, x_ref):
                    copy.start()

        def put(row, value):
            xb_ref[row] = jnp.broadcast_to(value, (8, W))

        def take_halos(sweep, x_ref):
            for copy in columns(sweep):
                copy.wait_recv()
            for p in range(SB):
                put((p + 1) * EXT, col_recv[sweep, 0, p : p + 1, :])
                put((p + 1) * EXT + CB + 1, col_recv[sweep, 1, p : p + 1, :])

            @pl.when(has_lo)
            def _():
                for copy in upward(sweep, x_ref):
                    copy.wait_recv()
                for q in range(CB):
                    put(q + 1, row_recv[sweep, 0, q : q + 1, :])
                put(0, corn_recv[sweep, 0])
                put(CB + 1, corn_recv[sweep, 1])

            @pl.when(has_hi)
            def _():
                for copy in downward(sweep, x_ref):
                    copy.wait_recv()
                top = (SB + 1) * EXT
                for q in range(CB):
                    put(top + q + 1, row_recv[sweep, 1, q : q + 1, :])
                put(top, corn_recv[sweep, 2])
                put(top + CB + 1, corn_recv[sweep, 3])

        def drain_halos(sweep, x_ref):
            for copy in columns(sweep):
                copy.wait_send()

            @pl.when(has_hi)
            def _():
                for copy in upward(sweep, x_ref):
                    copy.wait_send()

            @pl.when(has_lo)
            def _():
                for copy in downward(sweep, x_ref):
                    copy.wait_send()

        def put_own(p, x_ref):
            for q in range(CB):
                put((p + 1) * EXT + q + 1, x_ref[p, q : q + 1, :])

        def face_tables(faces_ref, onehot, mask):
            faces = jnp.concatenate([faces_ref[s : s + 1, :] for s in (0, 0, 1, 1)], axis=1)
            block = ((faces.astype(jnp.float32) + 0.5) * (1.0 / BLK)).astype(jnp.int32)
            parity = lax.rem(lax.broadcasted_iota(jnp.int32, (1, 4 * PF), 1), 2 * PF) >= PF
            cell = faces - block * BLK + jnp.where(parity, BLK, 0)
            rows = lax.broadcasted_iota(jnp.int32, (BLKS, 4 * PF), 0)
            mask[...] = jnp.where(rows == block, 1.0, 0.0)
            step = 128

            def fill(i, _):
                first = pl.multiple_of(i * step, step)
                lanes = lax.broadcasted_iota(jnp.int32, (step, 4 * PF), 0) + first
                onehot[pl.ds(first, step), :] = jnp.where(lanes == cell, 1.0, 0.0).astype(jnp.bfloat16)
                return 0

            lax.fori_loop(0, PAIR // step, fill, 0)

        def packs(sweep):
            return [
                pltpu.make_async_remote_copy(
                    src_ref=pack_send.at[sweep, side],
                    dst_ref=pack_recv.at[sweep, side],
                    send_sem=ps_sem.at[sweep, side],
                    recv_sem=pr_sem.at[sweep, side],
                    device_id=(target, sp, ch),
                    device_id_type=MESH,
                )
                for side, target in ((0, t_up), (1, t_dn))
            ]

        def send_packs(sweep, x_ref):
            pairs = [x_ref[:, :, m * PAIR : (m + 1) * PAIR].reshape(BLKS, PAIR) for m in range(NP)]
            picked = sum3(
                jnp.dot(
                    split3(jnp.concatenate(pairs, axis=0)), oh_src[...], preferred_element_type=jnp.float32
                )
            )
            for m in range(NP):
                row = jnp.sum(picked[m * BLKS : (m + 1) * BLKS] * mask_src[...], axis=0, keepdims=True)
                for side in (0, 1):
                    pack_send[sweep, side, m : m + 1, :] = row[:, side * 2 * PF : (side + 1) * 2 * PF]
            for copy in packs(sweep):
                copy.start()

        def take_packs(sweep):
            for copy in packs(sweep):
                copy.wait_recv()
            contrib = []
            for side in (0, 1):
                total = jnp.zeros((NV, PF), jnp.float32)
                for w in range(NV):
                    rows = pl.ds(side * NV * NV + w, NV, stride=NV)
                    coupling = jnp.concatenate([coef32_ref[c, rows, :] for c in range(PF // 128)], axis=1)
                    first = (w % 2) * PF
                    total = total + coupling * pack_recv[sweep, side, w // 2 : w // 2 + 1, first : first + PF]
                contrib.append(total)
            spread = []
            for m in range(NP):
                row = jnp.concatenate(
                    [contrib[s][2 * m + odd : 2 * m + odd + 1, :] for s in (0, 1) for odd in (0, 1)], axis=1
                )
                spread.append(mask_dst[...] * row)
            term = sum3(
                lax.dot_general(
                    split3(jnp.concatenate(spread, axis=0)),
                    oh_dst[...],
                    (((1,), (1,)), ((), ())),
                    preferred_element_type=jnp.float32,
                )
            )
            for m in range(NP):
                lanes = slice(m * PAIR, (m + 1) * PAIR)
                base_ref[:, :, lanes] = base_ref[:, :, lanes] - term[m * BLKS : (m + 1) * BLKS].reshape(
                    SB, CB, PAIR
                )

        def keep(slot, q, product):
            folded = product[:, :PAIR]
            for m in range(1, NP):
                folded = folded + product[:, m * PAIR : (m + 1) * PAIR]
            for c in range(PAIR // 128):
                g_ref[slot, c, q * 8 : q * 8 + NV, :] = folded[:, c * 128 : (c + 1) * 128]

        def variable(slot, v):
            rows = pl.ds(v, CB, stride=8)
            return jnp.concatenate([g_ref[slot, c, rows, :] for c in range(PAIR // 128)], axis=1)

        def flat(slot):
            low = lax.broadcasted_iota(jnp.int32, (CB, PAIR), 1) < BLK
            parts = []
            for m in range(NP):
                even = variable(slot, 2 * m)
                odd = variable(slot, 2 * m + 1)
                parts.append(
                    jnp.where(low, even, odd) + pltpu.roll(jnp.where(low, odd, even), BLK, axis=1)
                )
            return parts

        def tile_row(p):
            for q in range(CB):
                block = p * CB + q
                total = None
                for k in range(K):
                    code = cols_ref[block * K + k]
                    up = jnp.where(code >= 6, 2, jnp.where(code >= 3, 1, 0))
                    row = (p + up) * EXT + q + code - 3 * up
                    part = tiles_ref[block, k].astype(jnp.float32) * xb_ref[row, 0:NV, :]
                    total = part if total is None else total + part
                keep(0, q, total)
            for m, part in enumerate(flat(0)):
                lanes = slice(m * PAIR, (m + 1) * PAIR)
                base_ref[p, :, lanes] = source_ref[p, :, lanes] - part

        def update_row(p, x_ref, out_ref):
            for q in range(CB):
                keep(1, q, inv_ref[p * CB + q].astype(jnp.float32) * res_ref[p, q : q + 1, :])
            for m, part in enumerate(flat(1)):
                lanes = slice(m * PAIR, (m + 1) * PAIR)
                out_ref[p, :, lanes] = x_ref[p, :, lanes] + part

        def loop(body):
            def step(p, _):
                body(p)
                return 0

            lax.fori_loop(0, SB, step, 0)

        send_halos(0, x0_ref)
        loop(lambda p: send_own(0, p, x0_ref))

        @pl.when(jnp.logical_not(has_lo))
        def _():
            for q in range(EXT):
                xb_ref[q] = jnp.zeros((8, W), jnp.float32)

        @pl.when(jnp.logical_not(has_hi))
        def _():
            for q in range(EXT):
                xb_ref[(SB + 1) * EXT + q] = jnp.zeros((8, W), jnp.float32)

        face_tables(fsrc_ref, oh_src, mask_src)
        send_packs(0, x0_ref)
        loop(lambda p: put_own(p, x0_ref))
        face_tables(fdst_ref, oh_dst, mask_dst)
        for c in range(PF // 128):
            coef32_ref[c] = coef_ref[:, c * 128 : (c + 1) * 128].astype(jnp.float32)
        for load in loads:
            load.wait()
        inv_load.wait()
        take_halos(0, x0_ref)

        def first_tiles(p):
            tile_row(p)
            forward(0, p)

        loop(first_tiles)
        take_packs(0)

        def first_update(p):
            collect(0, p, x0_ref)
            spectral(0, p, x0_ref)
            update_row(p, x0_ref, x1_ref)
            send_own(1, p, x1_ref)
            put_own(p, x1_ref)

        loop(first_update)

        send_halos(1, x1_ref)
        send_packs(1, x1_ref)
        take_halos(1, x1_ref)

        def last_tiles(p):
            tile_row(p)
            forward(1, p)

        loop(last_tiles)
        take_packs(1)

        def last_update(p):
            collect(1, p, x1_ref)
            spectral(1, p, x1_ref)
            update_row(p, x1_ref, adj_ref)

        loop(last_update)

        for sweep, x_ref in ((0, x0_ref), (1, x1_ref)):
            loop(lambda p: drain(sweep, p))
            drain_halos(sweep, x_ref)
            for copy in packs(sweep):
                copy.wait_send()

    scratch = [
        pltpu.VMEM((BLKS, K, NV, W), jnp.bfloat16),
        pltpu.VMEM((BLKS, NV, W), jnp.bfloat16),
        pltpu.VMEM((SB, CB, W), jnp.float32),
        pltpu.VMEM(((SB + 2) * EXT, 8, W), jnp.float32),
        pltpu.VMEM((SB, CB, W), jnp.float32),
        pltpu.VMEM((2, PAIR // 128, CB * 8, 128), jnp.float32),
        pltpu.VMEM((PF // 128, 2 * NV * NV, 128), jnp.float32),
        pltpu.VMEM((PAIR, 4 * PF), jnp.bfloat16),
        pltpu.VMEM((PAIR, 4 * PF), jnp.bfloat16),
        pltpu.VMEM((BLKS, 4 * PF), jnp.float32),
        pltpu.VMEM((BLKS, 4 * PF), jnp.float32),
        pltpu.VMEM((SWEEPS, 2, half, SB, CB, W), jnp.float32),
        pltpu.VMEM((SWEEPS, 2, half - 1, SB, CB, W), jnp.float32),
        pltpu.VMEM((SWEEPS, 2, SB, W), jnp.float32),
        pltpu.VMEM((SWEEPS, 4, 1, W), jnp.float32),
        pltpu.VMEM((SWEEPS, 2, SB, W), jnp.float32),
        pltpu.VMEM((SWEEPS, 2, CB, W), jnp.float32),
        pltpu.VMEM((SWEEPS, 4, 1, W), jnp.float32),
        pltpu.VMEM((SWEEPS, 2, NP, 2 * PF), jnp.float32),
        pltpu.VMEM((SWEEPS, 2, NP, 2 * PF), jnp.float32),
        pltpu.SemaphoreType.DMA((SB + 1,)),
        pltpu.SemaphoreType.DMA((SWEEPS, 2, half, SB)),
        pltpu.SemaphoreType.DMA((SWEEPS, 2, half, SB)),
        pltpu.SemaphoreType.DMA((SWEEPS, 8)),
        pltpu.SemaphoreType.DMA((SWEEPS, 8)),
        pltpu.SemaphoreType.DMA((SWEEPS, 2)),
        pltpu.SemaphoreType.DMA((SWEEPS, 2)),
    ]
    return kernel, scratch


def solution(mesh):
    n_inst, n_span, n_chord = (mesh.shape[a] for a in ("inst", "span", "chord"))

    def per_device(adj_source, adj_start, tiles, tile_cols, inverse_diag, face_src, face_dst, lag_coef):
        _, SB, CB, W = adj_source.shape
        K = tiles.shape[3]
        PF = face_src.shape[1]
        kernel, scratch = make_kernel((SB, CB, W, K, PF), n_inst, n_span, n_chord)
        vmem = pl.BlockSpec(memory_space=pltpu.VMEM)
        out = jax.ShapeDtypeStruct((SB, CB, W), jnp.float32)
        adjoint, residual = pl.pallas_call(
            kernel,
            out_shape=(out, out),
            in_specs=[
                vmem,
                vmem,
                pl.BlockSpec(memory_space=pltpu.SMEM),
                vmem,
                vmem,
                vmem,
                pl.BlockSpec(memory_space=pl.ANY),
                pl.BlockSpec(memory_space=pl.ANY),
            ],
            out_specs=(vmem, vmem),
            scratch_shapes=scratch,
            compiler_params=pltpu.CompilerParams(
                collective_id=0, has_side_effects=True, vmem_limit_bytes=48 * 1024 * 1024
            ),
        )(
            adj_start[0],
            adj_source[0],
            tile_cols.reshape(-1),
            face_src,
            face_dst,
            lag_coef[0],
            tiles.reshape(SB * CB, K, NV, W),
            inverse_diag.reshape(SB * CB, NV, W),
        )
        return adjoint[None], residual[None]

    return jax.shard_map(
        per_device,
        mesh=mesh,
        in_specs=(
            P("inst", "span", "chord", None),
            P("inst", "span", "chord", None),
            P("inst", "span", "chord", None, None, None),
            P("span", "chord", None),
            P("inst", "span", "chord", None, None),
            P(None, ("span", "chord")),
            P(None, ("span", "chord")),
            P("inst", None, ("span", "chord")),
        ),
        out_specs=(P("inst", "span", "chord", None), P("inst", "span", "chord", None)),
        check_vma=False,
    )
```

time: 276 us -> 43.7 us (0.16); the launches traced: 273 us -> 43.5 us
  other arithmetic: 137 us -> 0 us
  local copies, waits for them, and re-layouts: 56.1 us -> 6.09 us
  blocking collectives: 42.8 us -> 0 us
  Pallas kernels: 0 us -> 36.7 us
  starting transfers between devices: 20.1 us -> 0 us
  waiting for transfers between devices: 9.85 us -> 0 us
  matrix products: 5.92 us -> 0 us
    scatter-add x4 -> x0, other arithmetic: 103 us -> none  [lag_apply(): term = term.at[target // BLK, :, target % BLK].add(contrib.T)]
    all_gather x2 -> x0, blocking collectives: 42.8 us -> none  [per_device(): lax.all_gather(state[None], 'inst', axis=0, tiled=True)]
    pallas_call x0 -> x1, Pallas kernels: none -> 36.7 us  [per_device(): pl.pallas_call(kernel, out_shape=(out, out), in_specs=[vmem, vmem, pl.Blo...]
    ppermute x12 -> x0, starting transfers between devices: 20.1 us -> none  [the longest x4 8.21 us: from_behind(): lax.ppermute(array, axis, [(i, (i + by) % peers) for i in range(peers)])]
    reduce_sum x10 -> x0, other arithmetic: 14.8 us -> none  [the longest x4 13.1 us: tile_product(): return jnp.sum(coupled, axis=(2, 4)).reshape(rows, cols, width)]
    add x6 -> x0, other arithmetic: 12.6 us -> none  [the longest x4 8.88 us: per_device(): state = state + precondition(own_inverse, residual)]
    reduce_sum x9 -> x0, local copies, waits for them, and re-layouts: 12.4 us -> none  [the longest x6 9.05 us: tile_product(): return jnp.sum(coupled, axis=(2, 4)).reshape(rows, cols, width)]
    gather x4 -> x0, local copies, waits for them, and re-layouts: 11.9 us -> none  [lag_pack(): return blocks[faces // BLK, :, faces % BLK].T]
  transfers between devices with their start and end apart: 12 -> 0, of which waited for: 4 -> 0; matrix products, arithmetic and copies ran while one was open for 52% -> 0% of each run, Pallas kernels for 0% -> 0%
where the time goes in v1:
time: 43.7 us; the launch traced here: 43.5 us
  Pallas kernels  36.7 us (84%)
  local copies, waits for them, and re-layouts  6.09 us (14%)
  between operations  0.74 us (2%)
    pallas_call x1, Pallas kernels, per_device(): pl.pallas_call(kernel, out_shape=(out, out), in_specs=[vmem, vmem, pl.Blo...  36.7 us
    unnamed x15, local copies, waits for them, and re-layouts  5.99 us

profile of v1, /device:TPU:0, one launch (start us, length us, event | category | flops | bytes accessed | tf_op | source)
XLA Modules:
  0.0 43.5 jit_solution(8572950107565458936)
XLA Ops:
  0.6 0.8 %copy.13 = s32[4,8,4]{2,1,0:T(8,128)S(1)} copy(s32[4,8,4]{1,2,0:T(4,128)} %param.11) | data formatting | bytes 1024 | tf_op args[3]
  1.4 0.1 reshape.13.cols_ref
  1.5 0.0 copy-start
  1.5 0.0 copy-start.1
  1.5 0.0 copy-start.2
  1.6 0.0 copy-start.3
  1.6 0.0 copy-start.4
  1.6 1.3 %copy.15 = bf16[1,4,8,6,1920]{4,3,2,1,0:T(8,128)(2,1)S(1)} copy(bf16[1,4,8,6,1920]{4,2,3,1,0:T(8,128)(2,1)} %param.12) | data formatting | bytes 1474560 | tf_op args[4]
  2.9 2.5 %copy.14 = bf16[1,4,8,4,6,1920]{5,4,3,2,1,0:T(8,128)(2,1)S(1)} copy(bf16[1,4,8,4,6,1920]{5,3,4,2,1,0:T(4,128)(2,1)} %param.10) | data formatting | bytes 5898240 | tf_op args[2]
  5.4 0.0 copy-done
  5.4 0.0 copy-done.1
  5.4 0.0 copy-done.2
  5.4 0.0 copy-done.3
  5.4 0.0 copy-done.4
  5.4 36.7 %shard_map.95 = (f32[4,8,1920]{2,1,0:T(8,128)S(1)}, f32[4,8,1920]{2,1,0:T(8,128)S(1)}) custom-call(f32[4,8,1920]{2,1,0:T(8,128)S(1)} %bitcast.9, f32[4,8,1920]{2,1,0:T(8,128)S(1)} %bitcast.10, s32[128]{0:T(128)S(1)} %reshape.13.cols_ref, s32[2,256]{1,0:T(2,128)S(1)} %copy-done.3, s32[2,256]{1,0:T(2,128)S(1)} %copy-done.4, bf16[72,256]{1,0:T(8,128)(2,1)S(1)} %bitcast.13, ...), custom_call_target="tpu_custom_call" | custom-call | tf_op jit(solution)/shard_map/pallas_call | solution.py:528
  42.1 0.7 %copy.18 = f32[1,4,8,1920]{3,2,1,0:T(8,128)} copy(f32[1,4,8,1920]{3,2,1,0:T(8,128)S(1)} %bitcast.12) | data formatting | bytes 491520
  42.8 0.7 %copy.19 = f32[1,4,8,1920]{3,2,1,0:T(8,128)} copy(f32[1,4,8,1920]{3,2,1,0:T(8,128)S(1)} %bitcast.11) | data formatting | bytes 491520
Async XLA Ops:
  1.5 3.9 %copy-start = (f32[1,4,8,1920]{3,2,1,0:T(8,128)S(1)}, f32[1,4,8,1920]{3,2,1,0:T(8,128)}, u32[]{:S(2)}) copy-start(f32[1,4,8,1920]{3,2,1,0:T(8,128)} %param.9) | copy-start | bytes 737284
  1.5 3.9 %copy-start.1 = (f32[1,4,8,1920]{3,2,1,0:T(8,128)S(1)}, f32[1,4,8,1920]{3,2,1,0:T(8,128)}, u32[]{:S(2)}) copy-start(f32[1,4,8,1920]{3,2,1,0:T(8,128)} %param.8) | copy-start | bytes 737284
  1.5 3.9 %copy-start.2 = (bf16[1,72,256]{2,1,0:T(8,128)(2,1)S(1)}, bf16[1,72,256]{2,1,0:T(8,128)(2,1)}, u32[]{:S(2)}) copy-start(bf16[1,72,256]{2,1,0:T(8,128)(2,1)} %param.15) | copy-start | bytes 110596
  1.6 3.9 %copy-start.3 = (s32[2,256]{1,0:T(2,128)S(1)}, s32[2,256]{1,0:T(2,128)}, u32[]{:S(2)}) copy-start(s32[2,256]{1,0:T(2,128)} %fsrc_ref.1) | copy-start | bytes 6148
  1.6 3.9 %copy-start.4 = (s32[2,256]{1,0:T(2,128)S(1)}, s32[2,256]{1,0:T(2,128)}, u32[]{:S(2)}) copy-start(s32[2,256]{1,0:T(2,128)} %fdst_ref.1) | copy-start | bytes 6148

commit v2 on v1

--- a/solution.py
+++ b/solution.py
@@ -368,47 +368,56 @@
                     SB, CB, PAIR
                 )
 
-        def keep(slot, q, product):
+        def fold(product):
             folded = product[:, :PAIR]
             for m in range(1, NP):
                 folded = folded + product[:, m * PAIR : (m + 1) * PAIR]
-            for c in range(PAIR // 128):
-                g_ref[slot, c, q * 8 : q * 8 + NV, :] = folded[:, c * 128 : (c + 1) * 128]
-
-        def variable(slot, v):
-            rows = pl.ds(v, CB, stride=8)
-            return jnp.concatenate([g_ref[slot, c, rows, :] for c in range(PAIR // 128)], axis=1)
-
-        def flat(slot):
+            return folded
+
+        def flat(variable):
             low = lax.broadcasted_iota(jnp.int32, (CB, PAIR), 1) < BLK
             parts = []
             for m in range(NP):
-                even = variable(slot, 2 * m)
-                odd = variable(slot, 2 * m + 1)
+                even, odd = variable(2 * m), variable(2 * m + 1)
                 parts.append(
                     jnp.where(low, even, odd) + pltpu.roll(jnp.where(low, odd, even), BLK, axis=1)
                 )
             return parts
 
         def tile_row(p):
+            slot = lax.broadcasted_iota(jnp.int32, (K, W), 0)
             for q in range(CB):
                 block = p * CB + q
-                total = None
+                operand = None
                 for k in range(K):
-                    code = cols_ref[block * K + k]
+                    code = cols_ref[p, k, q]
                     up = jnp.where(code >= 6, 2, jnp.where(code >= 3, 1, 0))
                     row = (p + up) * EXT + q + code - 3 * up
-                    part = tiles_ref[block, k].astype(jnp.float32) * xb_ref[row, 0:NV, :]
-                    total = part if total is None else total + part
-                keep(0, q, total)
-            for m, part in enumerate(flat(0)):
+                    got = xb_ref[row, 0:K, :]
+                    operand = got if operand is None else jnp.where(slot == k, got, operand)
+                for v in range(NV):
+                    folded = fold(tiles_ref[block, v].astype(jnp.float32) * operand)
+                    for c in range(PAIR // 128):
+                        g_ref[v, c, q * K : (q + 1) * K, :] = folded[:, c * 128 : (c + 1) * 128]
+
+            def variable(v):
+                pieces = []
+                for c in range(PAIR // 128):
+                    rows = [g_ref[v, c, pl.ds(k, CB, stride=K), :] for k in range(K)]
+                    pieces.append(sum(rows[1:], rows[0]))
+                return jnp.concatenate(pieces, axis=1)
+
+            for m, part in enumerate(flat(variable)):
                 lanes = slice(m * PAIR, (m + 1) * PAIR)
                 base_ref[p, :, lanes] = source_ref[p, :, lanes] - part
 
         def update_row(p, x_ref, out_ref):
-            for q in range(CB):
-                keep(1, q, inv_ref[p * CB + q].astype(jnp.float32) * res_ref[p, q : q + 1, :])
-            for m, part in enumerate(flat(1)):
+            residual = res_ref[p]
+
+            def variable(v):
+                return fold(inv_ref[p, v].astype(jnp.float32) * residual)
+
+            for m, part in enumerate(flat(variable)):
                 lanes = slice(m * PAIR, (m + 1) * PAIR)
                 out_ref[p, :, lanes] = x_ref[p, :, lanes] + part
 
@@ -484,12 +493,12 @@
                 copy.wait_send()
 
     scratch = [
-        pltpu.VMEM((BLKS, K, NV, W), jnp.bfloat16),
-        pltpu.VMEM((BLKS, NV, W), jnp.bfloat16),
+        pltpu.VMEM((BLKS, NV, K, W), jnp.bfloat16),
+        pltpu.VMEM((SB, NV, CB, W), jnp.bfloat16),
         pltpu.VMEM((SB, CB, W), jnp.float32),
         pltpu.VMEM(((SB + 2) * EXT, 8, W), jnp.float32),
         pltpu.VMEM((SB, CB, W), jnp.float32),
-        pltpu.VMEM((2, PAIR // 128, CB * 8, 128), jnp.float32),
+        pltpu.VMEM((NV, PAIR // 128, CB * K, 128), jnp.float32),
         pltpu.VMEM((PF // 128, 2 * NV * NV, 128), jnp.float32),
         pltpu.VMEM((PAIR, 4 * PF), jnp.bfloat16),
         pltpu.VMEM((PAIR, 4 * PF), jnp.bfloat16),
@@ -541,17 +550,17 @@
             out_specs=(vmem, vmem),
             scratch_shapes=scratch,
             compiler_params=pltpu.CompilerParams(
-                collective_id=0, has_side_effects=True, vmem_limit_bytes=48 * 1024 * 1024
+                collective_id=0, has_side_effects=True, vmem_limit_bytes=60 * 1024 * 1024
             ),
         )(
             adj_start[0],
             adj_source[0],
-            tile_cols.reshape(-1),
+            tile_cols.transpose(0, 2, 1),
             face_src,
             face_dst,
             lag_coef[0],
-            tiles.reshape(SB * CB, K, NV, W),
-            inverse_diag.reshape(SB * CB, NV, W),
+            tiles[0].transpose(0, 1, 3, 2, 4).reshape(SB * CB, NV, K, W),
+            inverse_diag[0].transpose(0, 2, 1, 3),
         )
         return adjoint[None], residual[None]
 

time: 43.7 us -> 40.5 us (0.927)
  local copies, waits for them, and re-layouts: 6.09 us -> 3.31 us
    unnamed x15 -> x2, local copies, waits for them, and re-layouts: 5.99 us -> 3.31 us
where the time goes in v2:
time: 40.5 us; the launch traced here: 40.3 us
  Pallas kernels  36.4 us (90%)
  local copies, waits for them, and re-layouts  3.31 us (8%)
  between operations  0.64 us (2%)
    pallas_call x1, Pallas kernels, per_device(): pl.pallas_call(kernel, out_shape=(out, out), in_specs=[vmem, vmem, pl.Blo...  36.4 us
    unnamed x2, local copies, waits for them, and re-layouts  3.31 us

profile of v2, /device:TPU:0, one launch (start us, length us, event | category | flops | bytes accessed | tf_op | source)
XLA Modules:
  0.0 40.3 jit_solution(12699991697708158770)
XLA Ops:
  0.6 36.4 %shard_map.95 = (f32[4,8,1920]{2,1,0:T(8,128)}, f32[4,8,1920]{2,1,0:T(8,128)}) custom-call(f32[4,8,1920]{2,1,0:T(8,128)} %bitcast.16, f32[4,8,1920]{2,1,0:T(8,128)} %bitcast.17, s32[4,4,8]{2,1,0:T(4,128)} %bitcast.21, s32[2,256]{1,0:T(2,128)} %fsrc_ref.1, s32[2,256]{1,0:T(2,128)} %fdst_ref.1, bf16[72,256]{1,0:T(8,128)(2,1)} %bitcast.20, ...), custom_call_target="tpu_custom_call" | custom-call | tf_op jit(solution)/shard_map/pallas_call | solution.py:537
  37.0 1.7 %copy.12 = f32[1,4,8,1920]{3,2,1,0:T(8,128)} copy(f32[1,4,8,1920]{3,2,1,0:T(8,128)} %bitcast.19) | data formatting | bytes 491520
  38.7 1.7 %copy.13 = f32[1,4,8,1920]{3,2,1,0:T(8,128)} copy(f32[1,4,8,1920]{3,2,1,0:T(8,128)} %bitcast.18) | data formatting | bytes 491520

commit v3 on v2

--- a/solution.py
+++ b/solution.py
@@ -28,17 +28,15 @@
     return rotor_rate * first - spectral_viscosity * second
 
 
-def split3(x):
+def split(x):
     high = x.astype(jnp.bfloat16)
-    rest = x - high.astype(jnp.float32)
-    middle = rest.astype(jnp.bfloat16)
-    low = (rest - middle.astype(jnp.float32)).astype(jnp.bfloat16)
-    return jnp.concatenate([high, middle, low], axis=0)
-
-
-def sum3(y):
-    n = y.shape[0] // 3
-    return (y[2 * n :] + y[n : 2 * n]) + y[:n]
+    low = (x - high.astype(jnp.float32)).astype(jnp.bfloat16)
+    return jnp.concatenate([high, low], axis=0)
+
+
+def join(y):
+    n = y.shape[0] // 2
+    return y[:n] + y[n:]
 
 
 def make_kernel(sizes, n_inst, n_span, n_chord):
@@ -52,9 +50,9 @@
     lag = n_inst // BLADES
 
     def kernel(
-        x0_ref, source_ref, cols_ref, fsrc_ref, fdst_ref, coef_ref, tiles_hbm, inv_hbm,
+        x0_ref, source_ref, cols_ref, fsrc_ref, fdst_ref, coef_ref, inv_ref, tiles_hbm,
         adj_ref, res_ref,
-        tiles_ref, inv_ref, x1_ref, xb_ref, base_ref, g_ref, coef32_ref, oh_src, oh_dst, mask_src, mask_dst,
+        tiles_ref, x1_ref, xb_ref, base_ref, g_ref, coef32_ref, oh_src, oh_dst, mask_src, mask_dst,
         gat_ref, sum_ref, col_send, corn_send, col_recv, row_recv, corn_recv, pack_send, pack_recv,
         load_sem, gs_sem, gr_sem, hs_sem, hr_sem, ps_sem, pr_sem,
     ):
@@ -68,6 +66,37 @@
         has_lo = sp > 0
         has_hi = sp < n_span - 1
 
+        barrier = pltpu.get_barrier_semaphore()
+
+        def greet(i, s, c):
+            pl.semaphore_signal(barrier, inc=1, device_id=(i, s, c), device_id_type=MESH)
+
+        count = 4 + 3 * jnp.where(has_lo, 1, 0) + 3 * jnp.where(has_hi, 1, 0)
+        greet(t_up, sp, ch)
+        greet(t_dn, sp, ch)
+        greet(t, sp, ch_up)
+        greet(t, sp, ch_dn)
+        if lag != 1:
+            count = count + jnp.where(t > 0, 1, 0) + jnp.where(t < n_inst - 1, 1, 0)
+
+            @pl.when(t > 0)
+            def _():
+                greet(t - 1, sp, ch)
+
+            @pl.when(t < n_inst - 1)
+            def _():
+                greet(t + 1, sp, ch)
+
+        @pl.when(has_lo)
+        def _():
+            for c in (ch, ch_up, ch_dn):
+                greet(t, sp - 1, c)
+
+        @pl.when(has_hi)
+        def _():
+            for c in (ch, ch_up, ch_dn):
+                greet(t, sp + 1, c)
+
         loads = []
         for p in range(SB):
             loads.append(
@@ -75,43 +104,8 @@
                     tiles_hbm.at[pl.ds(p * CB, CB)], tiles_ref.at[pl.ds(p * CB, CB)], load_sem.at[p]
                 )
             )
-        inv_load = pltpu.make_async_copy(inv_hbm, inv_ref, load_sem.at[SB])
         for load in loads:
             load.start()
-        inv_load.start()
-
-        barrier = pltpu.get_barrier_semaphore()
-
-        def greet(i, s, c):
-            pl.semaphore_signal(barrier, inc=1, device_id=(i, s, c), device_id_type=MESH)
-
-        count = 4 + 3 * jnp.where(has_lo, 1, 0) + 3 * jnp.where(has_hi, 1, 0)
-        greet(t_up, sp, ch)
-        greet(t_dn, sp, ch)
-        greet(t, sp, ch_up)
-        greet(t, sp, ch_dn)
-        if lag != 1:
-            count = count + jnp.where(t > 0, 1, 0) + jnp.where(t < n_inst - 1, 1, 0)
-
-            @pl.when(t > 0)
-            def _():
-                greet(t - 1, sp, ch)
-
-            @pl.when(t < n_inst - 1)
-            def _():
-                greet(t + 1, sp, ch)
-
-        @pl.when(has_lo)
-        def _():
-            for c in (ch, ch_up, ch_dn):
-                greet(t, sp - 1, c)
-
-        @pl.when(has_hi)
-        def _():
-            for c in (ch, ch_up, ch_dn):
-                greet(t, sp + 1, c)
-
-        pl.semaphore_wait(barrier, count)
 
         def at(direction):
             return t if direction == RIGHT else n_inst - 1 - t
@@ -224,24 +218,27 @@
                 halo(sweep, 7, corn_send.at[sweep, 3], corn_recv.at[sweep, 3], (t, sp - 1, ch_dn)),
             ]
 
-        def send_halos(sweep, x_ref):
-            for p in range(SB):
-                col_send[sweep, 0, p : p + 1, :] = x_ref[p, CB - 1 : CB, :]
-                col_send[sweep, 1, p : p + 1, :] = x_ref[p, 0:1, :]
-            corn_send[sweep, 0] = x_ref[SB - 1, CB - 1 : CB, :]
-            corn_send[sweep, 1] = x_ref[SB - 1, 0:1, :]
-            corn_send[sweep, 2] = x_ref[0, CB - 1 : CB, :]
-            corn_send[sweep, 3] = x_ref[0, 0:1, :]
+        def stage_columns(sweep, p, x_ref):
+            col_send[sweep, 0, p] = x_ref[p, CB - 1 : CB, :]
+            col_send[sweep, 1, p] = x_ref[p, 0:1, :]
+
+        def send_columns(sweep):
             for copy in columns(sweep):
                 copy.start()
 
+        def send_up(sweep, x_ref):
             @pl.when(has_hi)
             def _():
+                corn_send[sweep, 0] = x_ref[SB - 1, CB - 1 : CB, :]
+                corn_send[sweep, 1] = x_ref[SB - 1, 0:1, :]
                 for copy in upward(sweep, x_ref):
                     copy.start()
 
+        def send_down(sweep, x_ref):
             @pl.when(has_lo)
             def _():
+                corn_send[sweep, 2] = x_ref[0, CB - 1 : CB, :]
+                corn_send[sweep, 3] = x_ref[0, 0:1, :]
                 for copy in downward(sweep, x_ref):
                     copy.start()
 
@@ -252,8 +249,8 @@
             for copy in columns(sweep):
                 copy.wait_recv()
             for p in range(SB):
-                put((p + 1) * EXT, col_recv[sweep, 0, p : p + 1, :])
-                put((p + 1) * EXT + CB + 1, col_recv[sweep, 1, p : p + 1, :])
+                put((p + 1) * EXT, col_recv[sweep, 0, p])
+                put((p + 1) * EXT + CB + 1, col_recv[sweep, 1, p])
 
             @pl.when(has_lo)
             def _():
@@ -292,22 +289,34 @@
             for q in range(CB):
                 put((p + 1) * EXT + q + 1, x_ref[p, q : q + 1, :])
 
-        def face_tables(faces_ref, onehot, mask):
+        def face_cells(faces_ref, mask):
             faces = jnp.concatenate([faces_ref[s : s + 1, :] for s in (0, 0, 1, 1)], axis=1)
             block = ((faces.astype(jnp.float32) + 0.5) * (1.0 / BLK)).astype(jnp.int32)
             parity = lax.rem(lax.broadcasted_iota(jnp.int32, (1, 4 * PF), 1), 2 * PF) >= PF
-            cell = faces - block * BLK + jnp.where(parity, BLK, 0)
             rows = lax.broadcasted_iota(jnp.int32, (BLKS, 4 * PF), 0)
             mask[...] = jnp.where(rows == block, 1.0, 0.0)
-            step = 128
+            return faces - block * BLK + jnp.where(parity, BLK, 0)
+
+        def source_table():
+            cell = face_cells(fsrc_ref, mask_src)
 
             def fill(i, _):
-                first = pl.multiple_of(i * step, step)
-                lanes = lax.broadcasted_iota(jnp.int32, (step, 4 * PF), 0) + first
-                onehot[pl.ds(first, step), :] = jnp.where(lanes == cell, 1.0, 0.0).astype(jnp.bfloat16)
+                first = pl.multiple_of(i * 128, 128)
+                lanes = lax.broadcasted_iota(jnp.int32, (128, 4 * PF), 0) + first
+                oh_src[pl.ds(first, 128), :] = jnp.where(lanes == cell, 1.0, 0.0).astype(jnp.bfloat16)
                 return 0
 
-            lax.fori_loop(0, PAIR // step, fill, 0)
+            lax.fori_loop(0, PAIR // 128, fill, 0)
+
+        def target_table():
+            cell = face_cells(fdst_ref, mask_dst).astype(jnp.float32)
+            lanes = lax.broadcasted_iota(jnp.int32, (128, 128), 1).astype(jnp.float32)
+            for j in range(0, 4 * PF, 128):
+                column = jnp.broadcast_to(cell[:, j : j + 128], (128, 128)).T
+                for c in range(0, PAIR, 128):
+                    oh_dst[j : j + 128, c : c + 128] = jnp.where(lanes + float(c) == column, 1.0, 0.0).astype(
+                        jnp.bfloat16
+                    )
 
         def packs(sweep):
             return [
@@ -324,9 +333,9 @@
 
         def send_packs(sweep, x_ref):
             pairs = [x_ref[:, :, m * PAIR : (m + 1) * PAIR].reshape(BLKS, PAIR) for m in range(NP)]
-            picked = sum3(
+            picked = join(
                 jnp.dot(
-                    split3(jnp.concatenate(pairs, axis=0)), oh_src[...], preferred_element_type=jnp.float32
+                    split(jnp.concatenate(pairs, axis=0)), oh_src[...], preferred_element_type=jnp.float32
                 )
             )
             for m in range(NP):
@@ -354,12 +363,9 @@
                     [contrib[s][2 * m + odd : 2 * m + odd + 1, :] for s in (0, 1) for odd in (0, 1)], axis=1
                 )
                 spread.append(mask_dst[...] * row)
-            term = sum3(
-                lax.dot_general(
-                    split3(jnp.concatenate(spread, axis=0)),
-                    oh_dst[...],
-                    (((1,), (1,)), ((), ())),
-                    preferred_element_type=jnp.float32,
+            term = join(
+                jnp.dot(
+                    split(jnp.concatenate(spread, axis=0)), oh_dst[...], preferred_element_type=jnp.float32
                 )
             )
             for m in range(NP):
@@ -384,9 +390,9 @@
                 )
             return parts
 
-        def tile_row(p):
+        def tile_blocks(p, blocks):
             slot = lax.broadcasted_iota(jnp.int32, (K, W), 0)
-            for q in range(CB):
+            for q in blocks:
                 block = p * CB + q
                 operand = None
                 for k in range(K):
@@ -398,12 +404,13 @@
                 for v in range(NV):
                     folded = fold(tiles_ref[block, v].astype(jnp.float32) * operand)
                     for c in range(PAIR // 128):
-                        g_ref[v, c, q * K : (q + 1) * K, :] = folded[:, c * 128 : (c + 1) * 128]
-
+                        g_ref[p, v, c, q * K : (q + 1) * K, :] = folded[:, c * 128 : (c + 1) * 128]
+
+        def finish_tiles(p):
             def variable(v):
                 pieces = []
                 for c in range(PAIR // 128):
-                    rows = [g_ref[v, c, pl.ds(k, CB, stride=K), :] for k in range(K)]
+                    rows = [g_ref[p, v, c, pl.ds(k, CB, stride=K), :] for k in range(K)]
                     pieces.append(sum(rows[1:], rows[0]))
                 return jnp.concatenate(pieces, axis=1)
 
@@ -421,15 +428,40 @@
                 lanes = slice(m * PAIR, (m + 1) * PAIR)
                 out_ref[p, :, lanes] = x_ref[p, :, lanes] + part
 
-        def loop(body):
+        def loop(body, first=0, last=SB):
             def step(p, _):
                 body(p)
                 return 0
 
-            lax.fori_loop(0, SB, step, 0)
-
-        send_halos(0, x0_ref)
-        loop(lambda p: send_own(0, p, x0_ref))
+            lax.fori_loop(first, last, step, 0)
+
+        inner = range(1, CB - 1)
+
+        def inner_tiles(p):
+            tile_blocks(p, inner)
+
+        def outer_tiles(sweep):
+            def end_row(i):
+                p = i * (SB - 1)
+                tile_blocks(p, range(CB))
+                finish_tiles(p)
+                forward(sweep, i)
+
+            def middle_row(p):
+                tile_blocks(p, (0, CB - 1))
+                finish_tiles(p)
+                forward(sweep, p + 1)
+
+            loop(end_row, 0, 2)
+            loop(middle_row, 1, SB - 1)
+
+        loop(lambda p: stage_columns(0, p, x0_ref))
+        pl.semaphore_wait(barrier, count)
+        loop(lambda p: send_own(0, p, x0_ref), 0, 1)
+        send_columns(0)
+        send_up(0, x0_ref)
+        send_down(0, x0_ref)
+        loop(lambda p: send_own(0, p, x0_ref), 1, SB)
 
         @pl.when(jnp.logical_not(has_lo))
         def _():
@@ -441,22 +473,17 @@
             for q in range(EXT):
                 xb_ref[(SB + 1) * EXT + q] = jnp.zeros((8, W), jnp.float32)
 
-        face_tables(fsrc_ref, oh_src, mask_src)
+        source_table()
         send_packs(0, x0_ref)
         loop(lambda p: put_own(p, x0_ref))
-        face_tables(fdst_ref, oh_dst, mask_dst)
+        for load in loads:
+            load.wait()
+        loop(inner_tiles, 1, SB - 1)
+        take_halos(0, x0_ref)
+        outer_tiles(0)
+        target_table()
         for c in range(PF // 128):
             coef32_ref[c] = coef_ref[:, c * 128 : (c + 1) * 128].astype(jnp.float32)
-        for load in loads:
-            load.wait()
-        inv_load.wait()
-        take_halos(0, x0_ref)
-
-        def first_tiles(p):
-            tile_row(p)
-            forward(0, p)
-
-        loop(first_tiles)
         take_packs(0)
 
         def first_update(p):
@@ -464,19 +491,25 @@
             spectral(0, p, x0_ref)
             update_row(p, x0_ref, x1_ref)
             send_own(1, p, x1_ref)
+            stage_columns(1, p, x1_ref)
+
+            @pl.when(p == 0)
+            def _():
+                send_down(1, x1_ref)
+
+            @pl.when(p == SB - 1)
+            def _():
+                send_columns(1)
+                send_up(1, x1_ref)
+
             put_own(p, x1_ref)
 
         loop(first_update)
 
-        send_halos(1, x1_ref)
         send_packs(1, x1_ref)
+        loop(inner_tiles, 1, SB - 1)
         take_halos(1, x1_ref)
-
-        def last_tiles(p):
-            tile_row(p)
-            forward(1, p)
-
-        loop(last_tiles)
+        outer_tiles(1)
         take_packs(1)
 
         def last_update(p):
@@ -494,26 +527,25 @@
 
     scratch = [
         pltpu.VMEM((BLKS, NV, K, W), jnp.bfloat16),
-        pltpu.VMEM((SB, NV, CB, W), jnp.bfloat16),
         pltpu.VMEM((SB, CB, W), jnp.float32),
         pltpu.VMEM(((SB + 2) * EXT, 8, W), jnp.float32),
         pltpu.VMEM((SB, CB, W), jnp.float32),
-        pltpu.VMEM((NV, PAIR // 128, CB * K, 128), jnp.float32),
+        pltpu.VMEM((SB, NV, PAIR // 128, CB * K, 128), jnp.float32),
         pltpu.VMEM((PF // 128, 2 * NV * NV, 128), jnp.float32),
         pltpu.VMEM((PAIR, 4 * PF), jnp.bfloat16),
-        pltpu.VMEM((PAIR, 4 * PF), jnp.bfloat16),
+        pltpu.VMEM((4 * PF, PAIR), jnp.bfloat16),
         pltpu.VMEM((BLKS, 4 * PF), jnp.float32),
         pltpu.VMEM((BLKS, 4 * PF), jnp.float32),
         pltpu.VMEM((SWEEPS, 2, half, SB, CB, W), jnp.float32),
         pltpu.VMEM((SWEEPS, 2, half - 1, SB, CB, W), jnp.float32),
-        pltpu.VMEM((SWEEPS, 2, SB, W), jnp.float32),
+        pltpu.VMEM((SWEEPS, 2, SB, 1, W), jnp.float32),
         pltpu.VMEM((SWEEPS, 4, 1, W), jnp.float32),
-        pltpu.VMEM((SWEEPS, 2, SB, W), jnp.float32),
+        pltpu.VMEM((SWEEPS, 2, SB, 1, W), jnp.float32),
         pltpu.VMEM((SWEEPS, 2, CB, W), jnp.float32),
         pltpu.VMEM((SWEEPS, 4, 1, W), jnp.float32),
         pltpu.VMEM((SWEEPS, 2, NP, 2 * PF), jnp.float32),
         pltpu.VMEM((SWEEPS, 2, NP, 2 * PF), jnp.float32),
-        pltpu.SemaphoreType.DMA((SB + 1,)),
+        pltpu.SemaphoreType.DMA((SB,)),
         pltpu.SemaphoreType.DMA((SWEEPS, 2, half, SB)),
         pltpu.SemaphoreType.DMA((SWEEPS, 2, half, SB)),
         pltpu.SemaphoreType.DMA((SWEEPS, 8)),
@@ -544,13 +576,13 @@
                 vmem,
                 vmem,
                 vmem,
-                pl.BlockSpec(memory_space=pl.ANY),
+                vmem,
                 pl.BlockSpec(memory_space=pl.ANY),
             ],
             out_specs=(vmem, vmem),
             scratch_shapes=scratch,
             compiler_params=pltpu.CompilerParams(
-                collective_id=0, has_side_effects=True, vmem_limit_bytes=60 * 1024 * 1024
+                collective_id=0, has_side_effects=True, vmem_limit_bytes=52 * 1024 * 1024
             ),
         )(
             adj_start[0],
@@ -559,8 +591,8 @@
             face_src,
             face_dst,
             lag_coef[0],
+            inverse_diag[0].transpose(0, 2, 1, 3),
             tiles[0].transpose(0, 1, 3, 2, 4).reshape(SB * CB, NV, K, W),
-            inverse_diag[0].transpose(0, 2, 1, 3),
         )
         return adjoint[None], residual[None]
 

time: 40.5 us -> 42.4 us (1.047)
  local copies, waits for them, and re-layouts: 3.31 us -> 7.21 us
  Pallas kernels: 36.4 us -> 34.1 us
    unnamed x2 -> x16, local copies, waits for them, and re-layouts: 3.31 us -> 7.21 us
    pallas_call x1, Pallas kernels: 36.4 us -> 34.1 us  [per_device(): pl.pallas_call(kernel, out_shape=(out, out), in_specs=[vmem, vmem, pl.Blo...]
where the time goes in v3:
time: 42.4 us; the launch traced here: 42 us
  Pallas kernels  34.1 us (80%)
  local copies, waits for them, and re-layouts  7.21 us (17%)
  between operations  0.66 us (2%)
    pallas_call x1, Pallas kernels, per_device(): pl.pallas_call(kernel, out_shape=(out, out), in_specs=[vmem, vmem, pl.Blo...  34.1 us
    unnamed x16, local copies, waits for them, and re-layouts  7.21 us

profile of v3, /device:TPU:0, one launch (start us, length us, event | category | flops | bytes accessed | tf_op | source)
XLA Modules:
  0.0 42.0 jit_solution(9054389182432923462)
XLA Ops:
  0.6 0.0 copy-start
  0.6 1.1 %copy-done = bf16[1,4,8,6,1920]{4,2,3,1,0:T(8,128)(2,1)S(1)} copy-done((bf16[1,4,8,6,1920]{4,2,3,1,0:T(8,128)(2,1)S(1)}, bf16[1,4,8,6,1920]{4,2,3,1,0:T(8,128)(2,1)}, u32[]{:S(2)}) %copy-start) | copy-done | bytes 737304
  1.7 0.0 copy-start.1
  1.8 0.9 %copy-done.1 = f32[1,4,8,1920]{3,2,1,0:T(8,128)S(1)} copy-done((f32[1,4,8,1920]{3,2,1,0:T(8,128)S(1)}, f32[1,4,8,1920]{3,2,1,0:T(8,128)}, u32[]{:S(2)}) %copy-start.1) | copy-done | bytes 245784
  2.7 0.0 copy-start.2
  2.7 0.9 %copy-done.2 = f32[1,4,8,1920]{3,2,1,0:T(8,128)S(1)} copy-done((f32[1,4,8,1920]{3,2,1,0:T(8,128)S(1)}, f32[1,4,8,1920]{3,2,1,0:T(8,128)}, u32[]{:S(2)}) %copy-start.2) | copy-done | bytes 245784
  3.6 0.0 copy-start.3
  3.6 0.8 %copy-done.3 = bf16[1,72,256]{2,1,0:T(8,128)(2,1)S(1)} copy-done((bf16[1,72,256]{2,1,0:T(8,128)(2,1)S(1)}, bf16[1,72,256]{2,1,0:T(8,128)(2,1)}, u32[]{:S(2)}) %copy-start.3) | copy-done | bytes 36888
  4.4 0.0 copy-start.4
  4.4 0.7 %copy-done.4 = s32[4,8,4]{1,2,0:T(4,128)S(1)} copy-done((s32[4,8,4]{1,2,0:T(4,128)S(1)}, s32[4,8,4]{1,2,0:T(4,128)}, u32[]{:S(2)}) %copy-start.4) | copy-done | bytes 536
  5.1 0.0 copy-start.5
  5.1 0.7 %copy-done.5 = s32[2,256]{1,0:T(2,128)S(1)} copy-done((s32[2,256]{1,0:T(2,128)S(1)}, s32[2,256]{1,0:T(2,128)}, u32[]{:S(2)}) %copy-start.5) | copy-done | bytes 2072
  5.8 0.0 copy-start.6
  5.8 0.7 %copy-done.6 = s32[2,256]{1,0:T(2,128)S(1)} copy-done((s32[2,256]{1,0:T(2,128)S(1)}, s32[2,256]{1,0:T(2,128)}, u32[]{:S(2)}) %copy-start.6) | copy-done | bytes 2072
  6.5 34.1 %shard_map.95 = (f32[4,8,1920]{2,1,0:T(8,128)S(1)}, f32[4,8,1920]{2,1,0:T(8,128)S(1)}) custom-call(f32[4,8,1920]{2,1,0:T(8,128)S(1)} %bitcast.15, f32[4,8,1920]{2,1,0:T(8,128)S(1)} %bitcast.16, s32[4,4,8]{2,1,0:T(4,128)S(1)} %bitcast.20, s32[2,256]{1,0:T(2,128)S(1)} %copy-done.5, s32[2,256]{1,0:T(2,128)S(1)} %copy-done.6, bf16[72,256]{1,0:T(8,128)(2,1)S(1)} %bitcast.19, ...), custom_call_target="tpu_custom_call" | custom-call | tf_op jit(solution)/shard_map/pallas_call | solution.py:569
  40.6 0.7 %copy.12 = f32[1,4,8,1920]{3,2,1,0:T(8,128)} copy(f32[1,4,8,1920]{3,2,1,0:T(8,128)S(1)} %bitcast.18) | data formatting | bytes 491520
  41.3 0.7 %copy.13 = f32[1,4,8,1920]{3,2,1,0:T(8,128)} copy(f32[1,4,8,1920]{3,2,1,0:T(8,128)S(1)} %bitcast.17) | data formatting | bytes 491520
Async XLA Ops:
  0.6 1.1 %copy-start = (bf16[1,4,8,6,1920]{4,2,3,1,0:T(8,128)(2,1)S(1)}, bf16[1,4,8,6,1920]{4,2,3,1,0:T(8,128)(2,1)}, u32[]{:S(2)}) copy-start(bf16[1,4,8,6,1920]{4,2,3,1,0:T(8,128)(2,1)} %param.12) | copy-start | bytes 2211844
  1.7 0.9 %copy-start.1 = (f32[1,4,8,1920]{3,2,1,0:T(8,128)S(1)}, f32[1,4,8,1920]{3,2,1,0:T(8,128)}, u32[]{:S(2)}) copy-start(f32[1,4,8,1920]{3,2,1,0:T(8,128)} %param.9) | copy-start | bytes 737284
  2.7 0.9 %copy-start.2 = (f32[1,4,8,1920]{3,2,1,0:T(8,128)S(1)}, f32[1,4,8,1920]{3,2,1,0:T(8,128)}, u32[]{:S(2)}) copy-start(f32[1,4,8,1920]{3,2,1,0:T(8,128)} %param.8) | copy-start | bytes 737284
  3.6 0.8 %copy-start.3 = (bf16[1,72,256]{2,1,0:T(8,128)(2,1)S(1)}, bf16[1,72,256]{2,1,0:T(8,128)(2,1)}, u32[]{:S(2)}) copy-start(bf16[1,72,256]{2,1,0:T(8,128)(2,1)} %param.15) | copy-start | bytes 110596
  4.4 0.7 %copy-start.4 = (s32[4,8,4]{1,2,0:T(4,128)S(1)}, s32[4,8,4]{1,2,0:T(4,128)}, u32[]{:S(2)}) copy-start(s32[4,8,4]{1,2,0:T(4,128)} %param.11) | copy-start | bytes 1540
  5.1 0.7 %copy-start.5 = (s32[2,256]{1,0:T(2,128)S(1)}, s32[2,256]{1,0:T(2,128)}, u32[]{:S(2)}) copy-start(s32[2,256]{1,0:T(2,128)} %fsrc_ref.1) | copy-start | bytes 6148
  5.8 0.7 %copy-start.6 = (s32[2,256]{1,0:T(2,128)S(1)}, s32[2,256]{1,0:T(2,128)}, u32[]{:S(2)}) copy-start(s32[2,256]{1,0:T(2,128)} %fdst_ref.1) | copy-start | bytes 6148
